TPU v7x, 32 devices: a whole 2x2x4 slice. The times are simulated.
32 devices in a mesh: fsdp: 16 (over z, y, core), rep: 2 (over x).
Axes of the slice: x: 2, y: 2, z: 4, core: 2. Of those that a mesh axis runs over, the one named last changes fastest.
Arguments:
- hidden_states: bfloat16 [64, 512, 768], P(('fsdp', 'rep')), may hold values from -6 to 6
- page_counts: int32 [64], P(('fsdp', 'rep')), may hold values from 128 to 512, as said below
- cotangent: bfloat16 [64, 512, 768], P(('fsdp', 'rep')), may hold values from -6 to 6
- attn_in_weight: bfloat16 [768, 2304], P('fsdp'), may hold values from -0.21875 to 0.21875
- attn_in_bias: bfloat16 [1536], P('fsdp'), may hold values from -3 to 3
- attn_out_weight: bfloat16 [768, 768], P('fsdp'), may hold values from -2 to 2
- attn_out_bias: bfloat16 [768], P('fsdp'), may hold values from -3 to 3
- first_gain: bfloat16 [768], P('fsdp'), may hold values from 0.099609375 to 1.8984375
- first_shift: bfloat16 [768], P('fsdp'), may hold values from -3 to 3
- up_weight: bfloat16 [768, 3072], P('fsdp'), may hold values from -0.21875 to 0.21875
- up_bias: bfloat16 [3072], P('fsdp'), may hold values from -3 to 3
- down_weight: bfloat16 [3072, 768], P('fsdp'), may hold values from -0.109375 to 0.109375
- down_bias: bfloat16 [768], P('fsdp'), may hold values from -3 to 3
- second_gain: bfloat16 [768], P('fsdp'), may hold values from 0.099609375 to 1.8984375
- second_shift: bfloat16 [768], P('fsdp'), may hold values from -3 to 3
Outputs:
- layer_output: bfloat16 [64, 512, 768], P(('fsdp', 'rep'))
- input_grad: bfloat16 [64, 512, 768], P(('fsdp', 'rep'))
- grad_attn_in_weight: float32 [768, 2304], P('fsdp')
- grad_attn_in_bias: float32 [1536], P('fsdp')
- grad_attn_out_weight: float32 [768, 768], P('fsdp')
- grad_attn_out_bias: float32 [768], P('fsdp')
- grad_first_gain: float32 [768], P('fsdp')
- grad_first_shift: float32 [768], P('fsdp')
- grad_up_weight: float32 [768, 3072], P('fsdp')
- grad_up_bias: float32 [3072], P('fsdp')
- grad_down_weight: float32 [3072, 768], P('fsdp')
- grad_down_bias: float32 [768], P('fsdp')
- grad_second_gain: float32 [768], P('fsdp')
- grad_second_shift: float32 [768], P('fsdp')
Inputs may be any that keep to these rules, and one draw needn't show every extreme that they name: The real tokens of a page fill its first page_counts slots; some page of every draw has all 512 slots real.
All inputs are finite; a program needn't handle non-finite values.
Results may differ from a plain program's by a relative error of at most 0.019.
Values may be sent and summed in bfloat16 or wider, within the bound.
No kernel may reach another device: no remote copies, remote signals or barrier semaphores. Data moves between devices by JAX's collectives and lax.ppermute only.
A program may use at most 128 MiB of HBM per device.

v0:
```python
import math

import jax
import jax.numpy as jnp
from jax import lax
from jax.experimental import pallas as pl
from jax.experimental.pallas import tpu as pltpu
from jax.sharding import PartitionSpec as P

HEADS = 12
BF = jnp.bfloat16
F32 = jnp.float32
NT = (((1,), (1,)), ((), ()))
TN = (((0,), (0,)), ((), ()))
CW = 384
THIRDS = 3
LINE = 4
TINY = 128
AXES = ("fsdp", "rep")


def dg(a, b, dims):
    return lax.dot_general(a, b, dims, preferred_element_type=F32)


def mm(a, b):
    return jnp.dot(a, b, preferred_element_type=F32)


def params():
    return pltpu.CompilerParams(vmem_limit_bytes=60 * 1024 * 1024)


def cost(us):
    return pl.CostEstimate(flops=int(us * 1.15e9), bytes_accessed=int(us * 1e6), transcendentals=0)


def flat_index(z, y, c, x):
    return (z * 4 + y * 2 + c) * 2 + x


def permutation(target):
    pairs = []
    for z in range(LINE):
        for y in range(2):
            for c in range(2):
                for x in range(2):
                    pairs.append((flat_index(z, y, c, x), flat_index(*target(z, y, c, x))))
    return pairs


def to_core(z, y, c, x):
    return (z, y, 1 - c, x)


def to_x(z, y, c, x):
    return (z, y, c, 1 - x)


def to_first(z, y, c, x):
    return (z, y, c, 1 - x) if c == 0 else (z, 1 - y, c, x)


def to_second(z, y, c, x):
    return (z, 1 - y, c, x) if c == 0 else (z, y, c, 1 - x)


def to_line(step):
    return lambda z, y, c, x: ((z + step) % LINE, y, c, x)


def move(value, target):
    return lax.ppermute(value, AXES, permutation(target))


def after(values, *earlier):
    return lax.optimization_barrier((values, earlier))[0]


def along_line(half):
    return [half] + [move(half, to_line(k)) for k in range(1, LINE)]


def in_order(parts):
    here = lax.axis_index("fsdp") // 4
    return jnp.stack([lax.select_n((here - chip) & (LINE - 1), *parts) for chip in range(LINE)])


def over_core(parts):
    return tuple(parts) + tuple(move(part, to_core) for part in parts)


def add_core(keep, got):
    keep, got = keep.astype(F32), got.astype(F32)
    return (keep[1] + got[1]).astype(BF), (keep[0] + got[0]).astype(BF)


def add_kernel(keep, got, go, stay):
    total = keep[...].astype(F32) + got[...].astype(F32)
    stay[...] = total[0].astype(BF)
    go[...] = total[1].astype(BF)


def add_wide(keep, got):
    _, second, line, rows, width = keep.shape
    half = line // 2
    both = pl.BlockSpec((2, 1, half, rows, width), lambda i, j: (0, i, j, 0, 0))
    one = pl.BlockSpec((1, half, rows, width), lambda i, j: (i, j, 0, 0))
    return pl.pallas_call(
        add_kernel,
        grid=(second, 2),
        in_specs=[both, both],
        out_specs=[one, one],
        out_shape=[jax.ShapeDtypeStruct(keep.shape[1:], BF)] * 2,
        compiler_params=params(),
        cost_estimate=cost(4),
        name="add_wide",
    )(keep, got)


def add_last(stay, got):
    return (stay.astype(F32) + got.astype(F32)).astype(BF)


def add_line(low, parts):
    total = low[0].astype(F32)
    for part in parts:
        total = total + part.astype(F32)
    return total.astype(BF)


def move_line(low):
    return [move(low[k], to_line(k)) for k in range(1, LINE)]


FIELDS = (((0, 0, 96), (4, 1, 192)), tuple((n, i, 48) for i, n in enumerate((1, 2, 3, 5, 6, 7))))


def rows_of(width):
    return [(i, at, min(TINY, width - at)) for i, at in enumerate(range(0, width, TINY))]


def pack_kernel(pos, inw, outw, upw, downw, *refs):
    vectors, (one, two, three) = refs[:8], refs[8:]

    def fill(x):
        third = inw.shape[1] // 3
        for t in range(THIRDS):
            for part in range(3):
                start = part * third + (2 * t + x) * 128
                piece = inw[:, start : start + 128]
                one[:, t * CW + part * 128 : t * CW + (part + 1) * 128] = piece
        row = lax.broadcasted_iota(jnp.int32, (48, TINY), 0)
        block = jnp.zeros((48, TINY), F32)
        for place, top, size in FIELDS[x]:
            for i, at, n in rows_of(size):
                piece = vectors[place][:, at : at + n].astype(F32)
                if n < TINY:
                    piece = jnp.concatenate([piece, jnp.zeros((1, TINY - n), F32)], axis=1)
                block = jnp.where(row == top + i, jnp.broadcast_to(piece, (48, TINY)), block)
        one[:, THIRDS * CW :] = block.astype(BF)
        two[:, :CW] = outw[:, x * CW : (x + 1) * CW]
        width = upw.shape[1] // 2
        two[:, CW:] = upw[:, x * width : (x + 1) * width]
        three[...] = downw[:, x * CW : (x + 1) * CW]

    @pl.when(pos[3] == 0)
    def _():
        fill(0)

    @pl.when(pos[3] == 1)
    def _():
        fill(1)


def pack(pos, weights, vectors):
    shapes = [
        (48, weights[0].shape[1] // 2 + TINY),
        (48, weights[1].shape[1] // 2 + weights[2].shape[1] // 2),
        (weights[3].shape[0], CW),
    ]
    arrays = tuple(weights) + tuple(v.reshape(1, -1) for v in vectors)
    full = lambda a: pl.BlockSpec(a, lambda i, p: (0, 0))
    return pl.pallas_call(
        pack_kernel,
        grid_spec=pltpu.PrefetchScalarGridSpec(
            num_scalar_prefetch=1,
            grid=(1,),
            in_specs=[full(a.shape) for a in arrays],
            out_specs=[full(a) for a in shapes],
        ),
        out_shape=[jax.ShapeDtypeStruct(a, BF) for a in shapes],
        compiler_params=params(),
        name="pack",
    )(pos, *arrays)


def sources(pos):
    y, c, x = pos[1], pos[2], pos[3]
    found = []
    for other in range(2):
        core = c ^ 1 if other else c
        swap = core == 0
        for first in range(2):
            for second in range(2):
                dx = jnp.where(swap, first, second)
                dy = jnp.where(swap, second, first)
                found.append((other * 4 + second * 2 + first, (y ^ dy) * 2 + core, x ^ dx))
    return found


def fetch(pos, buffers, target, rows, column, width, sem, stride=None, start=0):
    stride = width if stride is None else stride
    return [
        pltpu.make_async_copy(
            buffers[buffer].at[:, :, pl.ds(column, width)],
            target.at[
                :,
                pl.ds(pl.multiple_of(place * rows, 16), rows),
                pl.ds(pl.multiple_of(start + x * stride, 128), width),
            ],
            sem,
        )
        for buffer, place, x in sources(pos)
    ]


def fetch_in(pos, buffers, target, sem):
    copies = []
    for t in range(THIRDS):
        copies += fetch(pos, buffers, target, 48, t * CW, CW, sem, None, 2 * CW * t)
    return copies


def fetch_tiny(pos, buffers, target, column, sem):
    return [
        pltpu.make_async_copy(
            buffers[buffer].at[:, pl.ds(0, 16), pl.ds(column, TINY)], target.at[x, :, place], sem
        )
        for buffer, place, x in sources(pos)
    ]


def flat(ref, start=0, width=None):
    width = ref.shape[-1] if width is None else width
    return ref[:, :, start : start + width].reshape(-1, width) if len(ref.shape) == 3 else ref[:, start : start + width]


def run_all(copies):
    for copy in copies:
        copy.start()
    for copy in copies:
        copy.wait()


def spots(length, size, axis):
    shape = (length, TINY) if axis == 0 else (TINY, length)
    entry = lax.broadcasted_iota(jnp.int32, shape, axis).astype(F32)
    lane = lax.broadcasted_iota(jnp.int32, shape, 1 - axis).astype(F32)
    inner = entry - jnp.floor((entry + 0.5) * (1.0 / size)) * size
    return [
        jnp.where((lane + at == inner) & (lane < n), 1.0, 0.0).astype(BF) for _, at, n in rows_of(size)
    ]


def owned(shards, length):
    size = length // shards
    start = lax.broadcasted_iota(jnp.int32, (shards, length), 0) * size
    entry = lax.broadcasted_iota(jnp.int32, (shards, length), 1)
    return (entry >= start) & (entry < start + size)


def unpack_vectors(tiny, targets):
    shards = tiny.shape[1] * tiny.shape[2]
    made = {}
    for half in range(2):
        for place, top, size in FIELDS[half]:
            total = shards * size
            if size not in made:
                made[size] = spots(total, size, 1), owned(shards, total)
            each, mask = made[size]
            tiled = sum(mm(tiny[half, :, :, top + i, :].reshape(shards, TINY), spot) for i, spot in enumerate(each))
            targets[place][...] = jnp.sum(jnp.where(mask, tiled, 0.0), axis=0, keepdims=True)


def place_tile(pos, held, keep, send, rows, line):
    z, y, c, x = pos[0], pos[1], pos[2], pos[3]
    for relative, out in enumerate((keep, send)):
        core = c ^ relative
        swap = core == 0
        for first in range(2):
            for second in range(2):
                dx = jnp.where(swap, first, second)
                dy = jnp.where(swap, second, first)
                for slot, chip in line:
                    shard = chip * 4 + (y ^ dy) * 2 + core
                    start = pl.multiple_of(shard * rows, 16)
                    out[first, second, slot] = held[x ^ dx, pl.ds(start, rows), :]


def whole_line(pos):
    return [(k, (pos[0] + k) & (LINE - 1)) for k in range(LINE)]


def hold(held, tile):
    width = tile.shape[1] // 2
    held[0] = tile[:, :width].astype(BF)
    held[1] = tile[:, width:].astype(BF)


def joined(refs):
    return jnp.concatenate([r[...] for r in refs], axis=1)


def tiny_rows(vectors, fields):
    rows = []
    made = {}
    for vector, (_, _, size) in zip(vectors, fields):
        length = vector.shape[1]
        if size not in made:
            made[size] = spots(length, size, 0), owned(16, length)
        each, mask = made[size]
        own = jnp.where(mask, jnp.broadcast_to(vector, mask.shape), 0.0).astype(BF)
        rows += [mm(own, spot) for spot in each]
    count = len(rows)
    rows = jnp.concatenate(rows + [jnp.zeros((16 * (8 - count), TINY), F32)], axis=0).astype(BF)
    to = lax.broadcasted_iota(jnp.int32, (16 * 48, 128), 0)
    of = lax.broadcasted_iota(jnp.int32, (16 * 48, 128), 1)
    lift = jnp.where(to == (of & 15) * 48 + (of >> 4), 1.0, 0.0).astype(BF)
    return mm(lift, rows).astype(BF)


def grad_in_kernel(pos, x, *refs):
    parts, (keep, send, held) = refs[:-3], refs[-3:]
    for i, ref in enumerate(parts):

        @pl.when(pl.program_id(0) == i)
        def _(ref=ref):
            hold(held, dg(x[...], ref[...], TN))

    place_tile(pos, held, keep, send, 48, whole_line(pos))


def grad_last_kernel(pos, x, part, *refs):
    bq, bv, refs = refs[:THIRDS], refs[THIRDS : 2 * THIRDS], refs[2 * THIRDS :]
    upb, outb, g1, s1, downb, g2, s2, keep, send, held = refs
    hold(held, dg(x[...], part[...], TN))
    take = lambda ref: ref.at[:, :, :, :, pl.ds(0, CW)]
    place_tile(pos, held, take(keep), take(send), 48, whole_line(pos))
    groups = ((joined((*bq, *bv)), upb[...]), [r[...] for r in (outb, g1, s1, downb, g2, s2)])
    for half in range(2):
        held[half, :, :TINY] = tiny_rows(groups[half], FIELDS[half])
    take = lambda ref: ref.at[:, :, :, :, pl.ds(CW, TINY)]
    place_tile(pos, held.at[:, :, pl.ds(0, TINY)], take(keep), take(send), 48, whole_line(pos))


def grad_call(kernel, name, pos, arrays, in_specs, grid, block, shape, index, us):
    held = (2, 16 * 48, CW)
    return pl.pallas_call(
        kernel,
        grid_spec=pltpu.PrefetchScalarGridSpec(
            num_scalar_prefetch=1,
            grid=(grid,),
            in_specs=in_specs,
            out_specs=[pl.BlockSpec(block, index)] * 2,
            scratch_shapes=[pltpu.VMEM(held, BF)],
        ),
        out_shape=[jax.ShapeDtypeStruct(shape, BF)] * 2,
        compiler_params=params(),
        cost_estimate=cost(us),
        name=name,
    )(pos, *arrays)


def whole(array):
    return pl.BlockSpec(array.shape, lambda j, p: (0,) * array.ndim)


def grad_in(pos, x, parts):
    return grad_call(
        grad_in_kernel, "grad_in", pos, (x, *parts), [whole(a) for a in (x, *parts)], len(parts),
        (2, 2, LINE, 48, CW), (2, 2, LINE, 48, CW * len(parts)), lambda j, p: (0, 0, 0, 0, j), 5,
    )


def grad_last(pos, x, part, vectors):
    arrays = (x, part, *vectors)
    shape = (2, 2, LINE, 48, CW + TINY)
    return grad_call(
        grad_last_kernel, "grad_last", pos, arrays, [whole(a) for a in arrays], 1,
        shape, shape, lambda j, p: (0, 0, 0, 0, 0), 4,
    )


def halves(pos, mine, got):
    swap = pos[3] == 0
    return jnp.where(swap, mine, got).astype(F32), jnp.where(swap, got, mine).astype(F32)


def finish_down_kernel(pos, mine, got, down):
    for x, half in enumerate(halves(pos, mine[...], got[...])):
        down[:, CW * x : CW * (x + 1)] = half


def finish_kernel(pos, mine_u, got_u, mine, got, mine_last, got_last, out, up, weight, *vectors):
    width = up.shape[1] // 2
    third = weight.shape[1] // 3
    for x, half in enumerate(halves(pos, mine_u[...], got_u[...])):
        out[:, CW * x : CW * (x + 1)] = half[:, :CW]
        up[:, width * x : width * (x + 1)] = half[:, CW:]
    more = halves(pos, mine[...], got[...])
    for x, last in enumerate(halves(pos, mine_last[...], got_last[...])):
        for t in range(THIRDS):
            for part in range(3):
                start = part * third + (2 * t + x) * 128
                if t < THIRDS - 1:
                    piece = more[x][:, t * CW + part * 128 : t * CW + (part + 1) * 128]
                else:
                    piece = last[:, part * 128 : (part + 1) * 128]
                weight[:, start : start + 128] = piece
        for place, top, size in FIELDS[x]:
            for i, at, n in rows_of(size):
                vectors[place][:, at : at + n] = last[top + i : top + i + 1, CW : CW + n]


def finish(kernel, name, pos, sums, shapes):
    full = lambda shape: pl.BlockSpec(shape, lambda i, p: (0, 0))
    return pl.pallas_call(
        kernel,
        grid_spec=pltpu.PrefetchScalarGridSpec(
            num_scalar_prefetch=1,
            grid=(1,),
            in_specs=[full(a.shape) for a in sums],
            out_specs=[full(shape) for shape in shapes],
        ),
        out_shape=[jax.ShapeDtypeStruct(shape, F32) for shape in shapes],
        compiler_params=params(),
        name=name,
    )(pos, *sums)


def pair_bias(bias):
    model = bias.shape[1] // 2
    parts = []
    for pair in range(model // 128):
        at = pair * 128
        parts += [bias[:, at : at + 128], jnp.zeros((1, 128), F32), bias[:, model + at : model + at + 128]]
    return jnp.concatenate(parts, axis=1)


def qkv_rows(x, weight, bias, outs):
    y = mm(x[...], flat(weight))
    scale = 1.0 / math.sqrt(x.shape[1] // HEADS)
    for t, out in enumerate(outs):
        width = out.shape[1]
        for at in range(0, width, 128):
            here = y[:, t * width + at : t * width + at + 128]
            place = t * width + at
            if at // 128 % 3 != 1:
                here = here + bias[:, place : place + 128]
            here = here.astype(BF)
            out[:, at : at + 128] = here * jnp.asarray(scale, BF) if at // 128 % 3 == 0 else here


def qkv_fetch_kernel(pos, x, *refs):
    buffers, outs, refs = refs[:8], refs[8 : 8 + THIRDS], refs[8 + THIRDS :]
    vectors, (weight, tiny, bias, sem, sem_tiny) = refs[:8], refs[8:]

    @pl.when(pl.program_id(0) == 0)
    def _():
        copies = fetch_in(pos, buffers, weight, sem)
        small = fetch_tiny(pos, buffers, tiny, THIRDS * CW, sem_tiny)
        for copy in small + copies:
            copy.start()
        for copy in small:
            copy.wait()
        unpack_vectors(tiny, vectors)
        bias[...] = pair_bias(vectors[0][...])
        for copy in copies:
            copy.wait()

    qkv_rows(x, weight, bias, outs)


def qkv_fetch(pos, x, buffers, shards, block=256):
    tokens, model = x.shape
    vec = lambda n: (pl.BlockSpec((1, n), lambda i, p: (0, 0)), jax.ShapeDtypeStruct((1, n), F32))
    vecs = [vec(model * n) for n in (2, 1, 1, 1, 4, 1, 1, 1)]
    return pl.pallas_call(
        qkv_fetch_kernel,
        grid_spec=pltpu.PrefetchScalarGridSpec(
            num_scalar_prefetch=1,
            grid=(tokens // block,),
            in_specs=[pl.BlockSpec((block, model), lambda i, p: (i, 0))]
            + [pl.BlockSpec(memory_space=pl.ANY)] * 8,
            out_specs=[pl.BlockSpec((block, 2 * CW), lambda i, p: (i, 0))] * THIRDS + [v[0] for v in vecs],
            scratch_shapes=[
                pltpu.VMEM((LINE, model // LINE, 3 * model), BF),
                pltpu.VMEM((2, LINE, shards // LINE, 16, TINY), BF),
                pltpu.VMEM((1, 3 * model), F32),
                pltpu.SemaphoreType.DMA,
                pltpu.SemaphoreType.DMA,
            ],
        ),
        out_shape=[jax.ShapeDtypeStruct((tokens, 2 * CW), BF)] * THIRDS + [v[1] for v in vecs],
        compiler_params=params(),
        cost_estimate=cost(10),
        name="qkv_fetch",
    )(pos, x, *buffers)


def qkv_plain_kernel(x, weight, bias, *outs):
    qkv_rows(x, weight, bias, outs)


def qkv(x, weight, bias, block=256):
    tokens, model = x.shape
    full = lambda a: pl.BlockSpec(a.shape, lambda i: (0, 0))
    return pl.pallas_call(
        qkv_plain_kernel,
        grid=(tokens // block,),
        in_specs=[pl.BlockSpec((block, model), lambda i: (i, 0)), full(weight), full(bias)],
        out_specs=[pl.BlockSpec((block, 2 * CW), lambda i: (i, 0))] * THIRDS,
        out_shape=[jax.ShapeDtypeStruct((tokens, 2 * CW), BF)] * THIRDS,
        compiler_params=params(),
    )(x, weight, bias)


def aug(q,k,h,bias,lane):
    own=(lane>=64) if h else (lane<64)
    j0=0 if h else 64
    z=jnp.zeros_like(q)
    one=jnp.where(lane==j0,jnp.ones_like(q),z)
    qa=jnp.where(own,q,one)
    ka=jnp.where(own,k,jnp.where(lane==j0,bias,z))
    return qa,ka,own
def attn_fwd_kernel(cnt,q_ref,k_ref,v_ref,o_ref,l_ref):
    p=pl.program_id(0)
    q=q_ref[...];k=k_ref[...];v=v_ref[...]
    S=q.shape[0]
    lane=lax.broadcasted_iota(jnp.int32,q.shape,1)
    row=lax.broadcasted_iota(jnp.int32,q.shape,0)
    bias=jnp.where(row<cnt[p],0.0,-1e30).astype(BF)
    vt=v.T
    outs=[]
    for h in range(2):
        qa,ka,own=aug(q,k,h,bias,lane)
        s=dg(ka,qa,NT)
        m=jnp.max(s,axis=0,keepdims=True)
        e=jnp.exp(s-m)
        l=jnp.sum(e,axis=0,keepdims=True)
        ot=mm(vt[64*h:64*h+64],e.astype(BF))
        outs.append(ot*(1.0/l))
        l_ref[0,0,h:h+1,:]=m+jnp.log(l)
    o_ref[...]=jnp.concatenate(outs,axis=0).T.astype(BF)
def attn_fwd(rows, counts, pages):
    tokens, width = rows.shape
    length, pairs = tokens // pages, width // CW
    block = lambda o: pl.BlockSpec((length, 128), lambda p, h, c: (p, 3 * h + o))
    return pl.pallas_call(
        attn_fwd_kernel,
        grid_spec=pltpu.PrefetchScalarGridSpec(
            num_scalar_prefetch=1,
            grid=(pages, pairs),
            in_specs=[block(0), block(1), block(2)],
            out_specs=[
                pl.BlockSpec((length, 128), lambda p, h, c: (p, h)),
                pl.BlockSpec((1, 1, 2, length), lambda p, h, c: (p, h, 0, 0)),
            ],
        ),
        out_shape=[
            jax.ShapeDtypeStruct((tokens, pairs * 128), BF),
            jax.ShapeDtypeStruct((pages, pairs, 2, length), F32),
        ],
        compiler_params=params(),
        cost_estimate=cost(3.5 * pairs),
        name="attn_fwd",
    )(counts, rows, rows, rows)


def attn_bwd_kernel(cnt,q_ref,k_ref,v_ref,g_ref,o_ref,l_ref,d_ref,bq_ref,bv_ref):
    p=pl.program_id(1)
    q=q_ref[...];k=k_ref[...];v=v_ref[...];g=g_ref[...]
    lane=lax.broadcasted_iota(jnp.int32,q.shape,1)
    row=lax.broadcasted_iota(jnp.int32,q.shape,0)
    bias=jnp.where(row<cnt[p],0.0,-1e30).astype(BF)
    prod=g.astype(F32)*o_ref[...].astype(F32)
    hi=prod.astype(BF); lo=(prod-hi.astype(F32)).astype(BF)
    r8=lax.broadcasted_iota(jnp.int32,(16,128),0); l8=lax.broadcasted_iota(jnp.int32,(16,128),1)
    sel=jnp.where(r8==l8//64,1.0,0.0).astype(BF)
    delta=dg(sel,hi,NT)+dg(sel,lo,NT)
    kt=k.T
    dv=[];dk=[];dqt=[]
    for h in range(2):
        qa,ka,own=aug(q,k,h,bias,lane)
        s=dg(ka,qa,NT)
        pr=jnp.exp(s-l_ref[0,0,h:h+1,:])
        va=jnp.where(own,v,jnp.zeros_like(v))
        dp=dg(va,g,NT)
        ds=(pr*(dp-delta[h:h+1])).astype(BF)
        dv.append(mm(pr.astype(BF),g)); dk.append(mm(ds,q))
        dqt.append(mm(kt[64*h:64*h+64],ds))
    first=lane<64
    dvv=jnp.where(first,dv[0],dv[1])
    dq=jnp.concatenate(dqt,axis=0).T*0.125
    d_ref[:,:128]=dq.astype(BF); d_ref[:,256:]=dvv.astype(BF)
    d_ref[:,128:256]=jnp.where(first,dk[0],dk[1]).astype(BF)
    sq=jnp.sum(dq,axis=0,keepdims=True); sv=jnp.sum(dvv,axis=0,keepdims=True)
    @pl.when(p==0)
    def _():
        bq_ref[...]=sq; bv_ref[...]=sv
    @pl.when(p>0)
    def _():
        bq_ref[...]+=sq; bv_ref[...]+=sv
def attn_bwd(rows, counts, grad, out, totals, pages, at):
    tokens, width = rows.shape
    length, pairs = tokens // pages, width // CW
    block = lambda o: pl.BlockSpec((length, 128), lambda h, p, c: (p, 3 * h + o))
    line = pl.BlockSpec((1, 128), lambda h, p, c: (0, h))
    return pl.pallas_call(
        attn_bwd_kernel,
        grid_spec=pltpu.PrefetchScalarGridSpec(
            num_scalar_prefetch=1,
            grid=(pairs, pages),
            in_specs=[
                block(0),
                block(1),
                block(2),
                pl.BlockSpec((length, 128), lambda h, p, c: (p, h + at)),
                pl.BlockSpec((length, 128), lambda h, p, c: (p, h)),
                pl.BlockSpec((1, 1, 2, length), lambda h, p, c: (p, h, 0, 0)),
            ],
            out_specs=[pl.BlockSpec((length, CW), lambda h, p, c: (p, h))] + [line] * 2,
        ),
        out_shape=[jax.ShapeDtypeStruct((tokens, width), BF)]
        + [jax.ShapeDtypeStruct((1, pairs * 128), F32)] * 2,
        compiler_params=params(),
        cost_estimate=cost(4.5 * pairs),
        name="attn_bwd",
    )(counts, rows, rows, rows, grad, out, totals)


def norm(t):
    m=jnp.mean(t,axis=-1,keepdims=True); c=t-m
    v=jnp.mean(c*c,axis=-1,keepdims=True); inv=lax.rsqrt(v+1e-12)
    return c*inv,inv
def norm_back(e,hat,inv):
    return inv*(e-jnp.mean(e,axis=-1,keepdims=True)-hat*jnp.mean(e*hat,axis=-1,keepdims=True))
def col(t): return jnp.sum(t,axis=0,keepdims=True)
C=768
def rows_at(ref, start, count):
    if len(ref.shape) == 2:
        return ref[start : start + count, :]
    each = ref.shape[1]
    return ref[start // each, start % each : start % each + count, :]


def main_fetch_kernel(pos, *refs):
    att, (x, cot), refs = refs[:-49], refs[-49:-47], refs[-47:]
    two, three, refs = refs[:8], refs[8:16], refs[16:]
    vecs, (out, gf, ga), sums, refs = refs[:7], refs[7:10], refs[10:17], refs[17:]
    keep_d, send_d, keep_u, send_u, refs = *refs[:4], refs[4:]
    slope, ow, uw, dw, big, wide, held, *sems = refs
    act, pre = big.at[0], big.at[1]
    low, back, first, attended = (wide.at[n] for n in range(4))
    step = pl.program_id(0)
    rows = x.shape[0]
    blocks = act.shape[0] // rows
    copies = (
        fetch(pos, two, ow, 48, 0, CW, sems[0]),
        fetch(pos, two, uw, 48, CW, uw.shape[2] // 2, sems[1]),
        fetch(pos, three, dw, dw.shape[1] // 4, 0, CW, sems[2]),
    )

    @pl.when(step == 0)
    def _():
        for group in copies:
            for copy in group:
                copy.start()

    def ready(place):
        @pl.when(step == 0)
        def _():
            for copy in copies[place]:
                copy.wait()

    @pl.when(step < blocks)
    def _():
        here = pl.ds(pl.multiple_of(step * rows, 16), rows)
        attended[here, :] = joined(att)
        main_kernel(
            att, x, cot, ow, uw, dw, *vecs, out,
            act.at[here, :], back.at[here, :], low.at[here, :], pre.at[here, :], first.at[here, :],
            gf, ga, *sums, slope, ready,
        )

    @pl.when((step >= blocks) & (step < blocks + LINE))
    def _():
        chip = (pos[0] + step - blocks) & (LINE - 1)
        columns = act.shape[1] // LINE
        here = pl.ds(pl.multiple_of(chip * columns, 128), columns)
        hold(held, dg(act[:, here], back[...], TN))
        place_tile(pos, held, keep_d, send_d, held.shape[1] // 4, [(0, 0)])

    @pl.when(step == blocks + LINE)
    def _():
        hold(held, dg(attended[...], first[...], TN))
        place_tile(pos, held, keep_u, send_u, 48, whole_line(pos))

    @pl.when(step > blocks + LINE)
    def _():
        at = pl.multiple_of((step - blocks - LINE - 1) * CW, 128)
        right = pl.multiple_of(at + pre.shape[1] // 2, 128)
        columns = jnp.concatenate([pre[:, pl.ds(at, CW)], pre[:, pl.ds(right, CW)]], axis=1)
        hold(held, dg(low[...], columns, TN))
        place_tile(pos, held, keep_u, send_u, 48, whole_line(pos))


def main_fetch(pos, att, x, cot, weights, vecs, rows=512):
    T, D = x.shape
    FF = vecs[3].shape[1]
    blocks, ups = T // rows, FF // 2 // CW
    rb = lambda n: pl.BlockSpec((rows, n), lambda i, p: (jnp.minimum(i, blocks - 1), 0))
    full = lambda a: pl.BlockSpec(a.shape, lambda i, p: (0, 0))
    vec = lambda n: (pl.BlockSpec((1, n), lambda i, p: (0, 0)), jax.ShapeDtypeStruct((1, n), F32))
    vs = [vec(n) for n in (D, D, D, FF, D, D, D)]
    down = pl.BlockSpec(
        (2, 2, 1, FF // 16, CW), lambda i, p: (0, 0, jnp.clip(i - blocks, 0, LINE - 1), 0, 0)
    )
    up = pl.BlockSpec(
        (2, 2, LINE, 48, CW), lambda i, p: (0, 0, 0, 0, jnp.clip(i - blocks - LINE, 0, ups))
    )
    shapes = [(2, 2, LINE, FF // 16, CW)] * 2 + [(2, 2, LINE, 48, CW * (1 + ups))] * 2
    return pl.pallas_call(
        main_fetch_kernel,
        grid_spec=pltpu.PrefetchScalarGridSpec(
            num_scalar_prefetch=1,
            grid=(blocks + LINE + 1 + ups,),
            in_specs=[rb(a.shape[1]) for a in (*att, x, cot)]
            + [pl.BlockSpec(memory_space=pl.ANY)] * len(weights)
            + [full(v) for v in vecs],
            out_specs=[rb(D)] * 3 + [v[0] for v in vs] + [down, down, up, up],
            scratch_shapes=[
                pltpu.VMEM((rows, FF), BF),
                pltpu.VMEM((LINE, D // LINE, D), BF),
                pltpu.VMEM((LINE, D // LINE, FF), BF),
                pltpu.VMEM((LINE, FF // LINE, D), BF),
                pltpu.VMEM((2, T, FF), BF),
                pltpu.VMEM((4, T, D), BF),
                pltpu.VMEM((2, 16 * 48, CW), BF),
            ]
            + [pltpu.SemaphoreType.DMA] * 3,
        ),
        out_shape=[jax.ShapeDtypeStruct((T, D), t) for t in (BF, F32, BF)]
        + [v[1] for v in vs]
        + [jax.ShapeDtypeStruct(a, BF) for a in shapes],
        compiler_params=params(),
        cost_estimate=cost(58),
        name="main",
    )(pos, *att, x, cot, *weights, *vecs)


def main_plain_kernel(*refs):
    main_kernel(refs[:-28], *refs[-28:])


def main_kernel(att,x,cot,ow,uw,dw,ob,g1,s1,ub,db,g2,s2,
                lo_ref,act_ref,sl_ref,nl_ref,pl_ref,fl_ref,gf_ref,ga_ref,
                vg2,vs2,vdb,vub,vg1,vs1,vob,slope,ready=lambda place: None):
    i=pl.program_id(0)
    FF=uw.shape[-1]
    ready(0)
    fs=x[...].astype(F32)+mm(joined(att),flat(ow))+ob[...]
    fh,fi=norm(fs)
    normed=fh*g1[...]+s1[...]
    nl=normed.astype(BF); nl_ref[...]=nl
    acc=normed+db[...]
    ready(1)
    for j in range(0,FF,C):
        pre=mm(nl,flat(uw,j,C))+ub[:,j:j+C]
        phi=0.5*(1.0+lax.erf(pre*(1.0/math.sqrt(2.0))))
        a=(pre*phi).astype(BF)
        act_ref[:,j:j+C]=a
        slope[:,j:j+C]=(phi+pre*jnp.exp(-0.5*pre*pre)*(1.0/math.sqrt(2.0*math.pi))).astype(slope.dtype)
        if j==0: ready(2)
        acc=acc+mm(a,rows_at(dw,j,C))
    sh,si=norm(acc)
    lo_ref[...]=(sh*g2[...]+s2[...]).astype(BF)
    gr=cot[...].astype(F32)
    gs=norm_back(gr*g2[...],sh,si)
    sl=gs.astype(BF); sl_ref[...]=sl
    gn=gs
    ubs=[]
    for j in range(0,FF,C):
        gp=dg(sl,rows_at(dw,j,C),NT)*slope[:,j:j+C]
        ubs.append(col(gp))
        gpl=gp.astype(BF); pl_ref[:,j:j+C]=gpl
        gn=gn+dg(gpl,flat(uw,j,C),NT)
    gf=norm_back(gn*g1[...],fh,fi)
    fl=gf.astype(BF); fl_ref[...]=fl; gf_ref[...]=gf
    ga_ref[...]=dg(fl,flat(ow),NT).astype(BF)
    vals=[(vg2,col(gr*sh)),(vs2,col(gr)),(vdb,col(gs)),(vub,jnp.concatenate(ubs,1)),(vg1,col(gn*fh)),(vs1,col(gn)),(vob,col(gf))]
    @pl.when(i==0)
    def _():
        for r,v in vals: r[...]=v
    @pl.when(i>0)
    def _():
        for r,v in vals: r[...]+=v
def main(att, x, cot, weights, vecs, R=256):
    T, D = x.shape
    FF = vecs[3].shape[1]
    rb = lambda n: pl.BlockSpec((R, n), lambda i: (i, 0))
    full = lambda a: pl.BlockSpec(a.shape, lambda i: (0, 0))
    sds = lambda n, t=BF: jax.ShapeDtypeStruct((T, n), t)
    vec = lambda n: (pl.BlockSpec((1, n), lambda i: (0, 0)), jax.ShapeDtypeStruct((1, n), F32))
    vs = [vec(n) for n in (D, D, D, FF, D, D, D)]
    return pl.pallas_call(
        main_plain_kernel,
        grid=(T // R,),
        in_specs=[rb(a.shape[1]) for a in (*att, x, cot)] + [full(w) for w in weights] + [full(v) for v in vecs],
        out_specs=[rb(D), rb(FF), rb(D), rb(D), rb(FF), rb(D), rb(D), rb(D)] + [v[0] for v in vs],
        out_shape=[sds(D), sds(FF), sds(D), sds(D), sds(FF), sds(D), sds(D, F32), sds(D)] + [v[1] for v in vs],
        scratch_shapes=[pltpu.VMEM((R, FF), F32)],
        compiler_params=params(),
        name="main",
    )(*att, x, cot, *weights, *vecs)


def tn_kernel(a,b,o): o[...]=dg(a[...],b[...],TN).astype(BF)
def tn(a,b,bm,bn):
    T,M=a.shape;N=b.shape[1]
    return pl.pallas_call(tn_kernel,grid=(M//bm,N//bn),
      in_specs=[pl.BlockSpec((T,bm),lambda i,j:(0,i)),pl.BlockSpec((T,bn),lambda i,j:(0,j))],
      out_specs=pl.BlockSpec((bm,bn),lambda i,j:(i,j)),out_shape=jax.ShapeDtypeStruct((M,N),BF),compiler_params=params())(a,b)
def ig_kernel(gf, parts, w, o):
    o[...] = (gf[...] + dg(joined(parts), flat(w), NT)).astype(BF)


def ig_plain_kernel(gf, *refs):
    ig_kernel(gf, refs[:-2], refs[-2], refs[-1])


def ig_fetch_kernel(pos, gf, *refs):
    parts, buffers, (o, weight, sem) = refs[:-11], refs[-11:-3], refs[-3:]

    @pl.when(pl.program_id(0) == 0)
    def _():
        run_all(fetch_in(pos, buffers, weight, sem))

    ig_kernel(gf, parts, weight, o)


def ig(parts, gf, weights, pos=None, R=256):
    T, D = gf.shape
    rb = lambda n: pl.BlockSpec((R, n), lambda i, *p: (i, 0))
    fetched = pos is not None
    return pl.pallas_call(
        ig_fetch_kernel if fetched else ig_plain_kernel,
        grid_spec=pltpu.PrefetchScalarGridSpec(
            num_scalar_prefetch=1 if fetched else 0,
            grid=(T // R,),
            in_specs=[rb(a.shape[1]) for a in (gf, *parts)]
            + [pl.BlockSpec(memory_space=pl.ANY) if fetched else pl.BlockSpec(w.shape, lambda i, *p: (0, 0)) for w in weights],
            out_specs=rb(D),
            scratch_shapes=[pltpu.VMEM((LINE, D // LINE, 3 * D), BF), pltpu.SemaphoreType.DMA] if fetched else [],
        ),
        out_shape=jax.ShapeDtypeStruct((T, D), BF),
        compiler_params=params(),
        cost_estimate=cost(10),
        name="ig",
    )(*([pos] if fetched else []), gf, *parts, *weights)


def local(
    hidden_states,
    page_counts,
    cotangent,
    attn_in_weight,
    attn_in_bias,
    attn_out_weight,
    attn_out_bias,
    first_gain,
    first_shift,
    up_weight,
    up_bias,
    down_weight,
    down_bias,
    second_gain,
    second_shift,
):
    pages, length, model = hidden_states.shape
    hidden = up_weight.shape[1]
    x = hidden_states.reshape(-1, model)
    grad_rows = cotangent.reshape(-1, model)
    weights = (attn_in_weight, attn_out_weight, up_weight, down_weight)
    vectors = (
        attn_in_bias,
        attn_out_bias,
        first_gain,
        first_shift,
        up_bias,
        down_bias,
        second_gain,
        second_shift,
    )
    lined = lax.axis_size("fsdp") == 4 * LINE and lax.axis_size("rep") == 2
    pairs = HEADS // 2 // THIRDS
    forward = [None] * THIRDS
    backward = [None] * THIRDS

    def ahead(t, rows):
        forward[t] = attn_fwd(rows, page_counts, pages)

    def back(t, rows):
        backward[t] = attn_bwd(rows, page_counts, grad_att, *forward[t], pages, pairs * t)

    if lined:
        index = lax.axis_index("fsdp")
        pos = jnp.stack([index // 4, index // 2 % 2, index % 2, lax.axis_index("rep")]).astype(jnp.int32)
        one, two, three = pack(pos, weights, vectors)
        line_one = in_order(along_line(one))
        second_one = move(line_one, to_second)
        first_one = move(line_one, to_first)
        parts_two = along_line(after(two, line_one))
        parts_three = along_line(after(three, line_one))
        both_one = move(after(second_one, *parts_two[1:]), to_first)
        in_w = over_core((line_one, first_one, second_one, both_one))
        line_two = in_order(parts_two)
        second_two = move(line_two, to_second)
        first_two = move(line_two, to_first)
        outs = qkv_fetch(pos, x, after(in_w, line_two), 16)
        rows, full = outs[:THIRDS], outs[THIRDS:]
        line_three = in_order(after(parts_three, rows))
        second_three = move(line_three, to_second)
        first_three = move(line_three, to_first)
        ahead(0, after(rows[0], line_three))
        both_two = move(after(second_two, forward[0]), to_first)
        ahead(1, after(rows[1], forward[0], second_two))
        both_three = move(after(second_three, forward[1]), to_first)
        ready = (line_two, first_two, second_two, line_three, first_three, second_three)
        ready = over_core(after(ready, forward[1]))
        ahead(2, after(rows[2], forward[1], second_three, first_three))
        last = over_core(after((both_two, both_three), forward[2]))
        later = (*ready[0:3], last[0], *ready[6:9], last[2], *ready[3:6], last[1], *ready[9:12], last[3])
    else:
        pos = None
        gathered = lambda a: lax.all_gather(a, "fsdp", axis=0, tiled=True)
        in_w = gathered(attn_in_weight).reshape(model, 3, -1, 128)
        in_w = (in_w.transpose(0, 2, 1, 3).reshape(model, 3 * model),)
        full = [gathered(v).astype(F32).reshape(1, -1) for v in vectors]
        later = tuple(gathered(w) for w in weights[1:])
        rows = qkv(x, in_w[0], pair_bias(full[0]))
        for t in range(THIRDS):
            ahead(t, rows[t])
    attended = [f[0] for f in forward]
    if lined:
        (
            output, grad_first, grad_att, vg2, vs2, vdb, vub, vg1, vs1, vob,
            keep_d, send_d, keep_u, send_u,
        ) = main_fetch(pos, attended, x, grad_rows, later, full[1:])
        core_d = move(send_d, to_core)
        core_u = move(send_u, to_core)
        back(0, rows[0])
        go_d, stay_d = add_wide(*after((keep_d, core_d), backward[0]))
        first_d = move(go_d, to_first)
        go_u, stay_u = add_wide(*after((keep_u, core_u), go_d))
        first_u = move(go_u, to_first)
        back(1, after(rows[1], go_u, stay_u))
        go_d, stay_d = add_core(*after((stay_d, first_d), backward[1]))
        second_d = move(go_d, to_second)
        keep_i, send_i = grad_in(pos, x, after((backward[0][0], backward[1][0]), go_d, stay_d))
        core_i = move(send_i, to_core)
        back(2, after(rows[2], keep_i))
        low_d = add_last(*after((stay_d, second_d), backward[2]))
        line_d = move_line(low_d)
        go_u, stay_u = add_core(*after((stay_u, first_u), low_d))
        second_u = move(go_u, to_second)
        parts = tuple(b[0] for b in backward)
        vbq = [b[1] for b in backward]
        vbv = [b[2] for b in backward]
        go_i, stay_i = add_wide(*after((keep_i, core_i), go_u, stay_u))
        first_i = move(go_i, to_first)
        keep_l, send_l = grad_last(
            pos, x, after(parts[2], go_i, stay_i), (*vbq, *vbv, vub, vob, vg1, vs1, vdb, vg2, vs2)
        )
        core_l = move(send_l, to_core)
        mine_d = add_line(low_d, after(line_d, keep_l))
        low_u = add_last(*after((stay_u, second_u), mine_d))
        line_u = move_line(low_u)
        go_l, stay_l = add_core(keep_l, after(core_l, low_u))
        first_l = move(go_l, to_first)
        go_i, stay_i = add_core(*after((stay_i, first_i), go_l, stay_l))
        second_i = move(go_i, to_second)
        input_grad = ig(parts, after(grad_first, go_i, stay_i), in_w, pos)
        mine_u = add_line(low_u, after(line_u, input_grad))
        low_i = add_last(*after((stay_i, second_i), mine_u))
        line_i = move_line(low_i)
        go_l, stay_l = add_core(*after((stay_l, first_l), low_i))
        second_l = move(go_l, to_second)
        got_d = move(after(mine_d, go_l), to_x)
        low_l = add_last(*after((stay_l, second_l), go_l))
        mine_i = add_line(low_i, after(line_i, low_l))
        line_l = move_line(after(low_l, mine_i))
        got_u = move(after(mine_u, mine_i), to_x)
        got_i = move(mine_i, to_x)
        (t_down,) = finish(
            finish_down_kernel, "finish_down", pos, (mine_d, after(got_d, low_l)), [down_weight.shape]
        )
        mine_l = add_line(low_l, after(line_l, t_down))
        got_l = move(mine_l, to_x)
        shapes = [attn_out_weight.shape, up_weight.shape, attn_in_weight.shape]
        shapes += [(1, v.shape[0]) for v in vectors]
        t_out, t_up, t_in, *small = finish(
            finish_kernel, "finish", pos, (mine_u, got_u, mine_i, got_i, mine_l, got_l), shapes
        )
        small = [b.reshape(-1) for b in small]
    else:
        (
            output, act, second_low, normed_low, pre_low, first_low, grad_first, grad_att,
            vg2, vs2, vdb, vub, vg1, vs1, vob,
        ) = main(attended, x, grad_rows, later, full[1:])
        for t in range(THIRDS):
            back(t, rows[t])
        parts = tuple(b[0] for b in backward)
        vbq = jnp.concatenate([b[1] for b in backward], axis=1)
        vbv = jnp.concatenate([b[2] for b in backward], axis=1)
        input_grad = ig(parts, grad_first, in_w)

        def total(a):
            share = lax.psum_scatter(a.astype(BF), "fsdp", scatter_dimension=0, tiled=True)
            return lax.psum(share, "rep").astype(F32)

        att = jnp.concatenate(attended, axis=1)
        t_down = total(tn(act, second_low, 768, 768))
        t_up = total(tn(normed_low, pre_low, 768, 768))
        t_out = total(tn(att, first_low, 768, 768))
        t_in = jnp.concatenate([tn(x, d, 768, 768) for d in parts], axis=1)
        t_in = total(t_in.reshape(model, -1, 3, 128).transpose(0, 2, 1, 3).reshape(model, 3 * model))
        small = [
            total(v.reshape(-1))
            for v in (jnp.concatenate([vbq, vbv], axis=1), vob, vg1, vs1, vub, vdb, vg2, vs2)
        ]
    b_in, b_out, b_g1, b_s1, b_up, b_down, b_g2, b_s2 = small
    return (
        output.reshape(hidden_states.shape),
        input_grad.reshape(hidden_states.shape),
        t_in, b_in, t_out, b_out, b_g1, b_s1, t_up, b_up, t_down, b_down, b_g2, b_s2,
    )


def solution(mesh):
    return jax.shard_map(
        local,
        mesh=mesh,
        in_specs=(
            P(("fsdp", "rep"), None, None),
            P(("fsdp", "rep")),
            P(("fsdp", "rep"), None, None),
            P("fsdp", None),
            P("fsdp"),
            P("fsdp", None),
            P("fsdp"),
            P("fsdp"),
            P("fsdp"),
            P("fsdp", None),
            P("fsdp"),
            P("fsdp", None),
            P("fsdp"),
            P("fsdp"),
            P("fsdp"),
        ),
        out_specs=(
            P(("fsdp", "rep"), None, None),
            P(("fsdp", "rep"), None, None),
            P("fsdp", None),
            P("fsdp"),
            P("fsdp", None),
            P("fsdp"),
            P("fsdp"),
            P("fsdp"),
            P("fsdp", None),
            P("fsdp"),
            P("fsdp", None),
            P("fsdp"),
            P("fsdp"),
            P("fsdp"),
        ),
        check_vma=False,
    )
```

profile of v0, /device:TPU:0, one launch (start us, length us, event | category | flops | bytes accessed | tf_op | source)
XLA Modules:
  0.0 286.3 jit_solution(6348680845008957599)
XLA Ops:
  5.3 5.1 %collective-permute-start.2 = (bf16[48,1280]{1,0:T(8,128)(2,1)}, bf16[48,1280]{1,0:T(8,128)(2,1)S(1)}, u32[]{:S(2)}, u32[]{:S(2)}) collective-permute-start(bf16[48,1280]{1,0:T(8,128)(2,1)} %get-tuple-element.150), channel_id=1, source_target_pairs={{0,24},{1,25},{2,26},{3,27},{4,28},{5,29},{6,30},{7,31},{8,0},{9,1... | collective-permute-start | bytes 368648 | tf_op jit(solution)/shard_map/ppermute | solution.py:73
  11.4 3.0 %collective-permute-done.2 = bf16[48,1280]{1,0:T(8,128)(2,1)S(1)} collective-permute-done((bf16[48,1280]{1,0:T(8,128)(2,1)}, bf16[48,1280]{1,0:T(8,128)(2,1)S(1)}, u32[]{:S(2)}, u32[]{:S(2)}) %collective-permute-start.2) | collective-permute-done | bytes 122912 | tf_op jit(solution)/shard_map/ppermute | solution.py:73
  14.4 6.8 %collective-permute-done.1 = bf16[48,1280]{1,0:T(8,128)(2,1)S(1)} collective-permute-done((bf16[48,1280]{1,0:T(8,128)(2,1)}, bf16[48,1280]{1,0:T(8,128)(2,1)S(1)}, u32[]{:S(2)}, u32[]{:S(2)}) %collective-permute-start.1) | collective-permute-done | bytes 122912 | tf_op jit(solution)/shard_map/ppermute | solution.py:73
  30.7 11.3 %collective-permute-done.6 = bf16[48,1920]{1,0:T(8,128)(2,1)S(1)} collective-permute-done((bf16[48,1920]{1,0:T(8,128)(2,1)S(1)}, bf16[48,1920]{1,0:T(8,128)(2,1)S(1)}, u32[]{:S(2)}, u32[]{:S(2)}) %collective-permute-start.6) | collective-permute-done | bytes 184352 | tf_op jit(solution)/shard_map/ppermute | solution.py:73
  43.2 7.7 %collective-permute-done.8.refs_3_.refs_6_ = bf16[4,48,1280]{2,1,0:T(8,128)(2,1)S(1)} collective-permute-done((bf16[4,48,1280]{2,1,0:T(8,128)(2,1)S(1)}, bf16[4,48,1280]{2,1,0:T(8,128)(2,1)S(1)}, u32[]{:S(2)}, u32[]{:S(2)}) %collective-permute-start.8) | collective-permute-done | bytes 491552 | tf_op jit(solution)/shard_map/ppermute | solution.py:73
  54.6 9.3 %qkv_fetch.1 = (bf16[1024,768]{1,0:T(8,128)(2,1)}, bf16[1024,768]{1,0:T(8,128)(2,1)}, bf16[1024,768]{1,0:T(8,128)(2,1)}, f32[1,1536]{1,0:T(1,128)}, f32[1,768]{1...) custom-call(s32[4]{0:T(128)} %pad_add_fusion.pos, ...), custom_call_target="tpu_custom_call" | custom-call | flops 11500000256 | bytes 10000000 | tf_op jit(solution)/shard_map/qkv_fetch/pallas_call | solution.py:489
  66.5 7.6 %attn_fwd.3 = (bf16[1024,256]{1,0:T(8,128)(2,1)}, f32[2,2,2,512]{3,2,1,0:T(2,128)}) custom-call(s32[2]{0:T(128)} %cnt.11, bf16[1024,768]{1,0:T(8,128)(2,1)} %get-tuple-element.171.q_ref.k_ref.v_ref, bf16[1024,768]{1,0:T(8,128)(2,1)} %get-tuple-element.171.q_ref.k_ref.v_ref, bf16[1024,768]{1,0:T(8,128)(2,1)} %get-tuple-element.171.q_ref.k_ref.v_ref), custom_call_target="tpu_custom_call" | custom-call | flops 8049999872 | bytes 7000000 | tf_op jit(solution)/shard_map/attn_fwd/pallas_call | solution.py:560
  74.8 7.6 %attn_fwd.4 = (bf16[1024,256]{1,0:T(8,128)(2,1)}, f32[2,2,2,512]{3,2,1,0:T(2,128)}) custom-call(s32[2]{0:T(128)} %cnt.11, bf16[1024,768]{1,0:T(8,128)(2,1)} %get-tuple-element.214.q_ref.k_ref.v_ref, bf16[1024,768]{1,0:T(8,128)(2,1)} %get-tuple-element.214.q_ref.k_ref.v_ref, bf16[1024,768]{1,0:T(8,128)(2,1)} %get-tuple-element.214.q_ref.k_ref.v_ref), custom_call_target="tpu_custom_call" | custom-call | flops 8049999872 | bytes 7000000 | tf_op jit(solution)/shard_map/attn_fwd/pallas_call | solution.py:560
  87.4 7.6 %attn_fwd.5 = (bf16[1024,256]{1,0:T(8,128)(2,1)}, f32[2,2,2,512]{3,2,1,0:T(2,128)}) custom-call(s32[2]{0:T(128)} %cnt.11, bf16[1024,768]{1,0:T(8,128)(2,1)} %get-tuple-element.225.q_ref.k_ref.v_ref, bf16[1024,768]{1,0:T(8,128)(2,1)} %get-tuple-element.225.q_ref.k_ref.v_ref, bf16[1024,768]{1,0:T(8,128)(2,1)} %get-tuple-element.225.q_ref.k_ref.v_ref), custom_call_target="tpu_custom_call" | custom-call | flops 8049999872 | bytes 7000000 | tf_op jit(solution)/shard_map/attn_fwd/pallas_call | solution.py:560
  95.3 3.5 %collective-permute-done.21.refs_16_ = bf16[4,192,384]{2,1,0:T(8,128)(2,1)} collective-permute-done((bf16[4,192,384]{2,1,0:T(8,128)(2,1)}, bf16[4,192,384]{2,1,0:T(8,128)(2,1)}, u32[]{:S(2)}, u32[]{:S(2)}) %collective-permute-start.21) | collective-permute-done | bytes 589856 | tf_op jit(solution)/shard_map/ppermute | solution.py:73
  105.0 61.0 %main.1 = (bf16[1024,768]{1,0:T(8,128)(2,1)}, f32[1024,768]{1,0:T(8,128)}, bf16[1024,768]{1,0:T(8,128)(2,1)}, f32[1,768]{1,0:T(1,128)}, f32[1,768]{1,0:T(1,128)}...) custom-call(s32[4]{0:T(128)} %pad_add_fusion.pos, ...), custom_call_target="tpu_custom_call" | custom-call | flops 66700001280 | bytes 58000000 | tf_op jit(solution)/shard_map/main/pallas_call | solution.py:734
  166.5 9.5 %attn_bwd.3 = (bf16[1024,768]{1,0:T(8,128)(2,1)}, f32[1,256]{1,0:T(1,128)}, f32[1,256]{1,0:T(1,128)}) custom-call(s32[2]{0:T(128)} %cnt.11, bf16[1024,768]{1,0:T(8,128)(2,1)} %get-tuple-element.171.q_ref.k_ref.v_ref, bf16[1024,768]{1,0:T(8,128)(2,1)} %get-tuple-element.171.q_ref.k_ref.v_ref, bf16[1024,768]{1,0:T(8,128)(2,1)} %get-tuple-element.171.q_ref.k_ref.v_ref, ...), custom_call_target="tpu_custom_call" | custom-call | flops 10350000128 | bytes 9000000 | tf_op jit(solution)/shard_map/attn_bwd/pallas_call | solution.py:620
  177.4 4.4 %add_wide.3 = (bf16[2,4,192,384]{3,2,1,0:T(8,128)(2,1)}, bf16[2,4,192,384]{3,2,1,0:T(8,128)(2,1)}) custom-call(bf16[2,2,4,192,384]{4,3,2,1,0:T(8,128)(2,1)} %get-tuple-element.207.keep, bf16[2,2,4,192,384]{4,3,2,1,0:T(8,128)(2,1)} %copy-done.16), custom_call_target="tpu_custom_call" | custom-call | flops 4600000000 | bytes 4000000 | tf_op jit(solution)/shard_map/add_wide/pallas_call | solution.py:109
  182.4 4.8 %add_wide.4 = (bf16[2,4,48,1920]{3,2,1,0:T(8,128)(2,1)}, bf16[2,4,48,1920]{3,2,1,0:T(8,128)(2,1)}) custom-call(bf16[2,2,4,48,1920]{4,3,2,1,0:T(8,128)(2,1)} %get-tuple-element.210.keep, bf16[2,2,4,48,1920]{4,3,2,1,0:T(8,128)(2,1)} %collective-permute-done.30.got), custom_call_target="tpu_custom_call" | custom-call | flops 4600000000 | bytes 4000000 | tf_op jit(solution)/shard_map/add_wide/pallas_call | solution.py:109
  188.7 9.7 %attn_bwd.4 = (bf16[1024,768]{1,0:T(8,128)(2,1)}, f32[1,256]{1,0:T(1,128)}, f32[1,256]{1,0:T(1,128)}) custom-call(s32[2]{0:T(128)} %cnt.11, bf16[1024,768]{1,0:T(8,128)(2,1)} %get-tuple-element.214.q_ref.k_ref.v_ref, bf16[1024,768]{1,0:T(8,128)(2,1)} %get-tuple-element.214.q_ref.k_ref.v_ref, bf16[1024,768]{1,0:T(8,128)(2,1)} %get-tuple-element.214.q_ref.k_ref.v_ref, ...), custom_call_target="tpu_custom_call" | custom-call | flops 10350000128 | bytes 9000000 | tf_op jit(solution)/shard_map/attn_bwd/pallas_call | solution.py:620
  200.0 7.3 %grad_in.1 = (bf16[2,2,4,48,768]{4,3,2,1,0:T(8,128)(2,1)}, bf16[2,2,4,48,768]{4,3,2,1,0:T(8,128)(2,1)}) custom-call(s32[4]{0:T(128)} %pad_add_fusion.pos, bf16[1024,768]{1,0:T(8,128)(2,1)} %bitcast.121, bf16[1024,768]{1,0:T(8,128)(2,1)} %get-tuple-element.221.refs_0_, bf16[1024,768]{1,0:T(8,128)(2,1)} %get-tuple-element.222.refs_1_), custom_call_target="tpu_custom_call" | custom-call | flops 5750000128 | bytes 5000000 | tf_op jit(solution)/shard_map/grad_in/pallas_call | solution.py:359
  207.3 9.5 %attn_bwd.5 = (bf16[1024,768]{1,0:T(8,128)(2,1)}, f32[1,256]{1,0:T(1,128)}, f32[1,256]{1,0:T(1,128)}) custom-call(s32[2]{0:T(128)} %cnt.11, bf16[1024,768]{1,0:T(8,128)(2,1)} %get-tuple-element.225.q_ref.k_ref.v_ref, bf16[1024,768]{1,0:T(8,128)(2,1)} %get-tuple-element.225.q_ref.k_ref.v_ref, bf16[1024,768]{1,0:T(8,128)(2,1)} %get-tuple-element.225.q_ref.k_ref.v_ref, ...), custom_call_target="tpu_custom_call" | custom-call | flops 10350000128 | bytes 9000000 | tf_op jit(solution)/shard_map/attn_bwd/pallas_call | solution.py:620
  217.0 3.3 %collective-permute-start.41 = (bf16[192,384]{1,0:T(8,128)(2,1)S(1)}, bf16[192,384]{1,0:T(8,128)(2,1)S(1)}, u32[]{:S(2)}, u32[]{:S(2)}) collective-permute-start(bf16[192,384]{1,0:T(8,128)(2,1)S(1)} %get-tuple-element.303), channel_id=1, source_target_pairs={{0,24},{1,25},{2,26},{3,27},{4,28},{5,29},{6,30},{7,31},{8,0},{9,1... | collective-permute-start | bytes 442376 | tf_op jit(solution)/shard_map/ppermute | solution.py:73
  223.2 3.8 %add_wide.5 = (bf16[2,4,48,768]{3,2,1,0:T(8,128)(2,1)}, bf16[2,4,48,768]{3,2,1,0:T(8,128)(2,1)}) custom-call(bf16[2,2,4,48,768]{4,3,2,1,0:T(8,128)(2,1)} %get-tuple-element.233.keep, bf16[2,2,4,48,768]{4,3,2,1,0:T(8,128)(2,1)} %collective-permute-done.33.got), custom_call_target="tpu_custom_call" | custom-call | flops 4600000000 | bytes 4000000 | tf_op jit(solution)/shard_map/add_wide/pallas_call | solution.py:109
  227.6 6.4 %grad_last.1 = (bf16[2,2,4,48,512]{4,3,2,1,0:T(8,128)(2,1)}, bf16[2,2,4,48,512]{4,3,2,1,0:T(8,128)(2,1)}) custom-call(s32[4]{0:T(128)} %pad_add_fusion.pos, bf16[1024,768]{1,0:T(8,128)(2,1)} %bitcast.122, bf16[1024,768]{1,0:T(8,128)(2,1)} %get-tuple-element.237.part.refs_2_, f32[1,256]{1,0:T(1,128)} %get-tuple-element.205.refs_0_, ...), custom_call_target="tpu_custom_call" | custom-call | flops 4600000000 | bytes 4000000 | tf_op jit(solution)/shard_map/grad_last/pallas_call | solution.py:359
  238.8 3.7 %collective-permute-start.44 = (bf16[48,1920]{1,0:T(8,128)(2,1)}, bf16[48,1920]{1,0:T(8,128)(2,1)S(1)}, u32[]{:S(2)}, u32[]{:S(2)}) collective-permute-start(bf16[48,1920]{1,0:T(8,128)(2,1)} %get-tuple-element.296), channel_id=1, source_target_pairs={{0,24},{1,25},{2,26},{3,27},{4,28},{5,29},{6,30},{7,31},{8,0},{9,1... | collective-permute-start | bytes 552968 | tf_op jit(solution)/shard_map/ppermute | solution.py:73
  246.5 10.1 %ig.1 = bf16[1024,768]{1,0:T(8,128)(2,1)} custom-call(s32[4]{0:T(128)} %pad_add_fusion.pos, f32[1024,768]{1,0:T(8,128)} %get-tuple-element.255.gf, bf16[1024,768]{1,0:T(8,128)(2,1)} %get-tuple-element.221.refs_0_, bf16[1024,768]{1,0:T(8,128)(2,1)} %get-tuple-element.222.refs_1_, bf16[1024,768]{1,0:T(8,128)(2,1)} %get-tuple-element.237.part.refs_2_, ...), custom_call_target="tpu_custom_call" | custom-call | flops 11500000256 | bytes 10000000 | tf_op jit(solution)/shard_map/ig/pallas_call | solution.py:857
  265.6 4.0 %collective-permute-done.47 = bf16[48,768]{1,0:T(8,128)(2,1)S(1)} collective-permute-done((bf16[48,768]{1,0:T(8,128)(2,1)S(1)}, bf16[48,768]{1,0:T(8,128)(2,1)S(1)}, u32[]{:S(2)}, u32[]{:S(2)}) %collective-permute-start.47) | collective-permute-done | bytes 73760 | tf_op jit(solution)/shard_map/ppermute | solution.py:73
  278.4 3.5 %collective-permute-done.57.got_last = bf16[48,512]{1,0:T(8,128)(2,1)S(1)} collective-permute-done((bf16[48,512]{1,0:T(8,128)(2,1)S(1)}, bf16[48,512]{1,0:T(8,128)(2,1)S(1)}, u32[]{:S(2)}, u32[]{:S(2)}) %collective-permute-start.57) | collective-permute-done | bytes 49184 | tf_op jit(solution)/shard_map/ppermute | solution.py:73
  (210 shorter events, 74.4 us)
Async XLA Ops:
  22.3 19.7 %collective-permute-start.4 = (bf16[4,48,1280]{2,1,0:T(8,128)(2,1)S(1)}, bf16[4,48,1280]{2,1,0:T(8,128)(2,1)S(1)}, u32[]{:S(2)}, u32[]{:S(2)}) collective-permute-start(bf16[4,48,1280]{2,1,0:T(8,128)(2,1)S(1)} %pad_maximum_fusion.2.refs_0_.refs_3_), channel_id=1, source_target_pairs={{0,4},{1,5},{2,3},{3,2},{4,0},{5,1},{6,7},{7,6},{8,12},{9,13},{10,... | collective-permute-start | bytes 1474568 | tf_op jit(solution)/shard_map/ppermute | solution.py:73
  25.5 16.4 %collective-permute-start.6 = (bf16[48,1920]{1,0:T(8,128)(2,1)S(1)}, bf16[48,1920]{1,0:T(8,128)(2,1)S(1)}, u32[]{:S(2)}, u32[]{:S(2)}) collective-permute-start(bf16[48,1920]{1,0:T(8,128)(2,1)S(1)} %copy-done.10), channel_id=1, source_target_pairs={{0,16},{1,17},{2,18},{3,19},{4,20},{5,21},{6,22},{7,23},{8,24},{9,... | collective-permute-start | bytes 552968 | tf_op jit(solution)/shard_map/ppermute | solution.py:73
  26.4 15.6 %collective-permute-start.5 = (bf16[48,1920]{1,0:T(8,128)(2,1)S(1)}, bf16[48,1920]{1,0:T(8,128)(2,1)S(1)}, u32[]{:S(2)}, u32[]{:S(2)}) collective-permute-start(bf16[48,1920]{1,0:T(8,128)(2,1)S(1)} %copy-done.10), channel_id=1, source_target_pairs={{0,8},{1,9},{2,10},{3,11},{4,12},{5,13},{6,14},{7,15},{8,16},{9,17... | collective-permute-start | bytes 552968 | tf_op jit(solution)/shard_map/ppermute | solution.py:73
  28.4 14.7 %collective-permute-start.3 = (bf16[4,48,1280]{2,1,0:T(8,128)(2,1)S(1)}, bf16[4,48,1280]{2,1,0:T(8,128)(2,1)S(1)}, u32[]{:S(2)}, u32[]{:S(2)}) collective-permute-start(bf16[4,48,1280]{2,1,0:T(8,128)(2,1)S(1)} %pad_maximum_fusion.2.refs_0_.refs_3_), channel_id=1, source_target_pairs={{0,1},{1,0},{2,6},{3,7},{4,5},{5,4},{6,2},{7,3},{8,9},{9,8},{10,14... | collective-permute-start | bytes 1474568 | tf_op jit(solution)/shard_map/ppermute | solution.py:73
  42.7 21.3 %collective-permute-start.15 = (bf16[192,384]{1,0:T(8,128)(2,1)S(1)}, bf16[192,384]{1,0:T(8,128)(2,1)S(1)}, u32[]{:S(2)}, u32[]{:S(2)}) collective-permute-start(bf16[192,384]{1,0:T(8,128)(2,1)S(1)} %copy-done.12), channel_id=1, source_target_pairs={{0,24},{1,25},{2,26},{3,27},{4,28},{5,29},{6,30},{7,31},{8,0},{9,1... | collective-permute-start | bytes 442376 | tf_op jit(solution)/shard_map/ppermute | solution.py:73
  52.4 32.9 %collective-permute-start.19 = (bf16[4,48,1920]{2,1,0:T(8,128)(2,1)S(1)}, bf16[4,48,1920]{2,1,0:T(8,128)(2,1)S(1)}, u32[]{:S(2)}, u32[]{:S(2)}) collective-permute-start(bf16[4,48,1920]{2,1,0:T(8,128)(2,1)S(1)} %pad_maximum_fusion.refs_5_), channel_id=1, source_target_pairs={{0,1},{1,0},{2,6},{3,7},{4,5},{5,4},{6,2},{7,3},{8,9},{9,8},{10,14... | collective-permute-start | bytes 2211848 | tf_op jit(solution)/shard_map/ppermute | solution.py:73
  53.1 21.1 %collective-permute-start.16 = (bf16[4,48,1920]{2,1,0:T(8,128)(2,1)S(1)}, bf16[4,48,1920]{2,1,0:T(8,128)(2,1)S(1)}, u32[]{:S(2)}, u32[]{:S(2)}) collective-permute-start(bf16[4,48,1920]{2,1,0:T(8,128)(2,1)S(1)} %pad_maximum_fusion.refs_5_), channel_id=1, source_target_pairs={{0,4},{1,5},{2,3},{3,2},{4,0},{5,1},{6,7},{7,6},{8,12},{9,13},{10,... | collective-permute-start | bytes 2211848 | tf_op jit(solution)/shard_map/ppermute | solution.py:73
  64.2 21.1 %collective-permute-start.18 = (bf16[4,192,384]{2,1,0:T(8,128)(2,1)S(1)}, bf16[4,192,384]{2,1,0:T(8,128)(2,1)}, u32[]{:S(2)}, u32[]{:S(2)}) collective-permute-start(bf16[4,192,384]{2,1,0:T(8,128)(2,1)S(1)} %pad_maximum_fusion.1.refs_13_), channel_id=1, source_target_pairs={{0,1},{1,0},{2,6},{3,7},{4,5},{5,4},{6,2},{7,3},{8,9},{9,8},{10,14... | collective-permute-start | bytes 1769480 | tf_op jit(solution)/shard_map/ppermute | solution.py:73
  65.8 19.5 %collective-permute-start.17 = (bf16[4,192,384]{2,1,0:T(8,128)(2,1)S(1)}, bf16[4,192,384]{2,1,0:T(8,128)(2,1)}, u32[]{:S(2)}, u32[]{:S(2)}) collective-permute-start(bf16[4,192,384]{2,1,0:T(8,128)(2,1)S(1)} %pad_maximum_fusion.1.refs_13_), channel_id=1, source_target_pairs={{0,4},{1,5},{2,3},{3,2},{4,0},{5,1},{6,7},{7,6},{8,12},{9,13},{10,... | collective-permute-start | bytes 1769480 | tf_op jit(solution)/shard_map/ppermute | solution.py:73
  74.1 20.9 %collective-permute-start.20 = (bf16[4,48,1920]{2,1,0:T(8,128)(2,1)S(1)}, bf16[4,48,1920]{2,1,0:T(8,128)(2,1)S(1)}, u32[]{:S(2)}, u32[]{:S(2)}) collective-permute-start(bf16[4,48,1920]{2,1,0:T(8,128)(2,1)S(1)} %collective-permute-done.16.refs_7_), channel_id=1, source_target_pairs={{0,1},{1,0},{2,6},{3,7},{4,5},{5,4},{6,2},{7,3},{8,9},{9,8},{10,14... | collective-permute-start | bytes 2211848 | tf_op jit(solution)/shard_map/ppermute | solution.py:73
  166.0 16.5 %collective-permute-start.30 = (bf16[2,2,4,48,1920]{4,3,2,1,0:T(8,128)(2,1)}, bf16[2,2,4,48,1920]{4,3,2,1,0:T(8,128)(2,1)}, u32[]{:S(2)}, u32[]{:S(2)}) collective-permute-start(bf16[2,2,4,48,1920]{4,3,2,1,0:T(8,128)(2,1)} %get-tuple-element.202), channel_id=1, source_target_pairs={{0,2},{1,3},{2,0},{3,1},{4,6},{5,7},{6,4},{7,5},{8,10},{9,11},{10,... | collective-permute-start | bytes 8847368 | tf_op jit(solution)/shard_map/ppermute | solution.py:73
  181.8 16.5 %collective-permute-start.32 = (bf16[2,4,192,384]{3,2,1,0:T(8,128)(2,1)}, bf16[2,4,192,384]{3,2,1,0:T(8,128)(2,1)S(1)}, u32[]{:S(2)}, u32[]{:S(2)}) collective-permute-start(bf16[2,4,192,384]{3,2,1,0:T(8,128)(2,1)} %get-tuple-element.209), channel_id=1, source_target_pairs={{0,1},{1,0},{2,6},{3,7},{4,5},{5,4},{6,2},{7,3},{8,9},{9,8},{10,14... | collective-permute-start | bytes 3538952 | tf_op jit(solution)/shard_map/ppermute | solution.py:73
  187.2 33.9 %collective-permute-start.34 = (bf16[2,4,48,1920]{3,2,1,0:T(8,128)(2,1)}, bf16[2,4,48,1920]{3,2,1,0:T(8,128)(2,1)S(1)}, u32[]{:S(2)}, u32[]{:S(2)}) collective-permute-start(bf16[2,4,48,1920]{3,2,1,0:T(8,128)(2,1)} %get-tuple-element.212), channel_id=1, source_target_pairs={{0,1},{1,0},{2,6},{3,7},{4,5},{5,4},{6,2},{7,3},{8,9},{9,8},{10,14... | collective-permute-start | bytes 4423688 | tf_op jit(solution)/shard_map/ppermute | solution.py:73
  199.1 17.8 %collective-permute-start.35 = (bf16[4,192,384]{2,1,0:T(8,128)(2,1)S(1)}, bf16[4,192,384]{2,1,0:T(8,128)(2,1)S(1)}, u32[]{:S(2)}, u32[]{:S(2)}) collective-permute-start(bf16[4,192,384]{2,1,0:T(8,128)(2,1)S(1)} %get-tuple-element.289), channel_id=1, source_target_pairs={{0,4},{1,5},{2,3},{3,2},{4,0},{5,1},{6,7},{7,6},{8,12},{9,13},{10,... | collective-permute-start | bytes 1769480 | tf_op jit(solution)/shard_map/ppermute | solution.py:73
  207.3 15.9 %collective-permute-start.33 = (bf16[2,2,4,48,768]{4,3,2,1,0:T(8,128)(2,1)}, bf16[2,2,4,48,768]{4,3,2,1,0:T(8,128)(2,1)}, u32[]{:S(2)}, u32[]{:S(2)}) collective-permute-start(bf16[2,2,4,48,768]{4,3,2,1,0:T(8,128)(2,1)} %get-tuple-element.224), channel_id=1, source_target_pairs={{0,2},{1,3},{2,0},{3,1},{4,6},{5,7},{6,4},{7,5},{8,10},{9,11},{10,... | collective-permute-start | bytes 3538952 | tf_op jit(solution)/shard_map/ppermute | solution.py:73
  217.0 18.4 %collective-permute-start.41 = (bf16[192,384]{1,0:T(8,128)(2,1)S(1)}, bf16[192,384]{1,0:T(8,128)(2,1)S(1)}, u32[]{:S(2)}, u32[]{:S(2)}) collective-permute-start(bf16[192,384]{1,0:T(8,128)(2,1)S(1)} %get-tuple-element.303), channel_id=1, source_target_pairs={{0,24},{1,25},{2,26},{3,27},{4,28},{5,29},{6,30},{7,31},{8,0},{9,1... | collective-permute-start | bytes 442376 | tf_op jit(solution)/shard_map/ppermute | solution.py:73
  220.3 15.1 %collective-permute-start.40 = (bf16[192,384]{1,0:T(8,128)(2,1)S(1)}, bf16[192,384]{1,0:T(8,128)(2,1)S(1)}, u32[]{:S(2)}, u32[]{:S(2)}) collective-permute-start(bf16[192,384]{1,0:T(8,128)(2,1)S(1)} %get-tuple-element.304), channel_id=1, source_target_pairs={{0,16},{1,17},{2,18},{3,19},{4,20},{5,21},{6,22},{7,23},{8,24},{9,... | collective-permute-start | bytes 442376 | tf_op jit(solution)/shard_map/ppermute | solution.py:73
  220.7 14.7 %collective-permute-start.39 = (bf16[192,384]{1,0:T(8,128)(2,1)S(1)}, bf16[192,384]{1,0:T(8,128)(2,1)}, u32[]{:S(2)}, u32[]{:S(2)}) collective-permute-start(bf16[192,384]{1,0:T(8,128)(2,1)S(1)} %get-tuple-element.305), channel_id=1, source_target_pairs={{0,8},{1,9},{2,10},{3,11},{4,12},{5,13},{6,14},{7,15},{8,16},{9,17... | collective-permute-start | bytes 442376 | tf_op jit(solution)/shard_map/ppermute | solution.py:73
  221.7 16.1 %collective-permute-start.38 = (bf16[4,48,1920]{2,1,0:T(8,128)(2,1)S(1)}, bf16[4,48,1920]{2,1,0:T(8,128)(2,1)S(1)}, u32[]{:S(2)}, u32[]{:S(2)}) collective-permute-start(bf16[4,48,1920]{2,1,0:T(8,128)(2,1)S(1)} %get-tuple-element.287), channel_id=1, source_target_pairs={{0,4},{1,5},{2,3},{3,2},{4,0},{5,1},{6,7},{7,6},{8,12},{9,13},{10,... | collective-permute-start | bytes 2211848 | tf_op jit(solution)/shard_map/ppermute | solution.py:73
  227.1 17.1 %collective-permute-start.36 = (bf16[2,4,48,768]{3,2,1,0:T(8,128)(2,1)}, bf16[2,4,48,768]{3,2,1,0:T(8,128)(2,1)S(1)}, u32[]{:S(2)}, u32[]{:S(2)}) collective-permute-start(bf16[2,4,48,768]{3,2,1,0:T(8,128)(2,1)} %get-tuple-element.236), channel_id=1, source_target_pairs={{0,1},{1,0},{2,6},{3,7},{4,5},{5,4},{6,2},{7,3},{8,9},{9,8},{10,14... | collective-permute-start | bytes 1769480 | tf_op jit(solution)/shard_map/ppermute | solution.py:73
  238.8 17.8 %collective-permute-start.44 = (bf16[48,1920]{1,0:T(8,128)(2,1)}, bf16[48,1920]{1,0:T(8,128)(2,1)S(1)}, u32[]{:S(2)}, u32[]{:S(2)}) collective-permute-start(bf16[48,1920]{1,0:T(8,128)(2,1)} %get-tuple-element.296), channel_id=1, source_target_pairs={{0,24},{1,25},{2,26},{3,27},{4,28},{5,29},{6,30},{7,31},{8,0},{9,1... | collective-permute-start | bytes 552968 | tf_op jit(solution)/shard_map/ppermute | solution.py:73
  242.6 16.4 %collective-permute-start.43 = (bf16[48,1920]{1,0:T(8,128)(2,1)}, bf16[48,1920]{1,0:T(8,128)(2,1)S(1)}, u32[]{:S(2)}, u32[]{:S(2)}) collective-permute-start(bf16[48,1920]{1,0:T(8,128)(2,1)} %get-tuple-element.297), channel_id=1, source_target_pairs={{0,16},{1,17},{2,18},{3,19},{4,20},{5,21},{6,22},{7,23},{8,24},{9,... | collective-permute-start | bytes 552968 | tf_op jit(solution)/shard_map/ppermute | solution.py:73
  243.3 15.7 %collective-permute-start.42 = (bf16[48,1920]{1,0:T(8,128)(2,1)S(1)}, bf16[48,1920]{1,0:T(8,128)(2,1)S(1)}, u32[]{:S(2)}, u32[]{:S(2)}) collective-permute-start(bf16[48,1920]{1,0:T(8,128)(2,1)S(1)} %get-tuple-element.298), channel_id=1, source_target_pairs={{0,8},{1,9},{2,10},{3,11},{4,12},{5,13},{6,14},{7,15},{8,16},{9,17... | collective-permute-start | bytes 552968 | tf_op jit(solution)/shard_map/ppermute | solution.py:73
  243.9 15.2 %collective-permute-start.49 = (bf16[2,4,48,512]{3,2,1,0:T(8,128)(2,1)S(1)}, bf16[2,4,48,512]{3,2,1,0:T(8,128)(2,1)S(1)}, u32[]{:S(2)}, u32[]{:S(2)}) collective-permute-start(bf16[2,4,48,512]{3,2,1,0:T(8,128)(2,1)S(1)} %get-tuple-element.291), channel_id=1, source_target_pairs={{0,1},{1,0},{2,6},{3,7},{4,5},{5,4},{6,2},{7,3},{8,9},{9,8},{10,14... | collective-permute-start | bytes 1179656 | tf_op jit(solution)/shard_map/ppermute | solution.py:73
  (67 other events, 598.2 us)
where the time goes:
time: 290 us; the launch traced here: 286 us
  Pallas kernels  167 us (58%)
  starting transfers between devices  51.8 us (18%)
  waiting for transfers between devices  51.8 us (18%)
  other arithmetic  7.79 us (3%)
  local copies, waits for them, and re-layouts  6.69 us (2%)
    pallas_call x1, Pallas kernels, main_fetch(): pl.pallas_call(main_fetch_kernel, grid_spec=pltpu.PrefetchScalarGridSpec(...  61 us
    ppermute x58, starting transfers between devices, move(): return lax.ppermute(value, AXES, permutation(target))  51.8 us
    ppermute x58, waiting for transfers between devices, move(): return lax.ppermute(value, AXES, permutation(target))  51.8 us
    pallas_call x3, Pallas kernels, attn_bwd(): pl.pallas_call(attn_bwd_kernel, grid_spec=pltpu.PrefetchScalarGridSpec(nu...  28.6 us
    pallas_call x3, Pallas kernels, attn_fwd(): pl.pallas_call(attn_fwd_kernel, grid_spec=pltpu.PrefetchScalarGridSpec(nu...  22.8 us
    pallas_call x2, Pallas kernels, grad_call(): pl.pallas_call(kernel, grid_spec=pltpu.PrefetchScalarGridSpec(num_scalar_...  13.7 us
    pallas_call x3, Pallas kernels, add_wide(): pl.pallas_call(add_kernel, grid=(second, 2), in_specs=[both, both], out_s...  13 us
    pallas_call x1, Pallas kernels, ig(): pl.pallas_call(ig_fetch_kernel if fetched else ig_plain_kernel, grid_spec...  10.1 us
  transfers between devices with their start and end apart: 58, of which 16 were waited for; matrix products, arithmetic and copies ran while one was open for 2% of the time, Pallas kernels for 35%

commit v1 on v0

--- a/solution.py
+++ b/solution.py
@@ -103,12 +103,11 @@
 
 def add_wide(keep, got):
     _, second, line, rows, width = keep.shape
-    half = line // 2
-    both = pl.BlockSpec((2, 1, half, rows, width), lambda i, j: (0, i, j, 0, 0))
-    one = pl.BlockSpec((1, half, rows, width), lambda i, j: (i, j, 0, 0))
+    both = pl.BlockSpec((2, 1, line, rows, width), lambda i: (0, i, 0, 0, 0))
+    one = pl.BlockSpec((1, line, rows, width), lambda i: (i, 0, 0, 0))
     return pl.pallas_call(
         add_kernel,
-        grid=(second, 2),
+        grid=(second,),
         in_specs=[both, both],
         out_specs=[one, one],
         out_shape=[jax.ShapeDtypeStruct(keep.shape[1:], BF)] * 2,
@@ -154,7 +153,7 @@
         block = jnp.zeros((48, TINY), F32)
         for place, top, size in FIELDS[x]:
             for i, at, n in rows_of(size):
-                piece = vectors[place][:, at : at + n].astype(F32)
+                piece = vectors[place][at : at + n].astype(F32).reshape(1, n)
                 if n < TINY:
                     piece = jnp.concatenate([piece, jnp.zeros((1, TINY - n), F32)], axis=1)
                 block = jnp.where(row == top + i, jnp.broadcast_to(piece, (48, TINY)), block)
@@ -179,8 +178,8 @@
         (48, weights[1].shape[1] // 2 + weights[2].shape[1] // 2),
         (weights[3].shape[0], CW),
     ]
-    arrays = tuple(weights) + tuple(v.reshape(1, -1) for v in vectors)
-    full = lambda a: pl.BlockSpec(a, lambda i, p: (0, 0))
+    arrays = tuple(weights) + tuple(vectors)
+    full = lambda a: pl.BlockSpec(a, lambda i, p: (0,) * len(a))
     return pl.pallas_call(
         pack_kernel,
         grid_spec=pltpu.PrefetchScalarGridSpec(
@@ -430,7 +429,7 @@
         grid_spec=pltpu.PrefetchScalarGridSpec(
             num_scalar_prefetch=1,
             grid=(1,),
-            in_specs=[full(a.shape) for a in sums],
+            in_specs=[pl.BlockSpec(memory_space=pltpu.VMEM)] * len(sums),
             out_specs=[full(shape) for shape in shapes],
         ),
         out_shape=[jax.ShapeDtypeStruct(shape, F32) for shape in shapes],
@@ -937,9 +936,11 @@
         both_two = move(after(second_two, forward[0]), to_first)
         ahead(1, after(rows[1], forward[0], second_two))
         both_three = move(after(second_three, forward[1]), to_first)
+        early = [move(part, to_core) for part in after((line_two,), forward[0])]
         ready = (line_two, first_two, second_two, line_three, first_three, second_three)
-        ready = over_core(after(ready, forward[1]))
-        ahead(2, after(rows[2], forward[1], second_three, first_three))
+        moved = [move(part, to_core) for part in after(ready[1:], forward[1])]
+        ahead(2, after(rows[2], forward[1], second_three, first_three, *early))
+        ready += (*early, *moved)
         last = over_core(after((both_two, both_three), forward[2]))
         later = (*ready[0:3], last[0], *ready[6:9], last[2], *ready[3:6], last[1], *ready[9:12], last[3])
     else:

time: 290 us -> 288 us (level)
  Pallas kernels: 167 us -> 164 us
  transfers between devices with their start and end apart: 58 -> 58, of which waited for: 16 -> 16; matrix products, arithmetic and copies ran while one was open for 2% -> 2% of each run, Pallas kernels for 35% -> 34%
where the time goes in v1:
time: 288 us; the launch traced here: 284 us
  Pallas kernels  164 us (57%)
  starting transfers between devices  53.6 us (19%)
  waiting for transfers between devices  51.4 us (18%)
  other arithmetic  7.79 us (3%)
  local copies, waits for them, and re-layouts  5.7 us (2%)
    pallas_call x1, Pallas kernels, main_fetch(): pl.pallas_call(main_fetch_kernel, grid_spec=pltpu.PrefetchScalarGridSpec(...  61.1 us
    ppermute x58, starting transfers between devices, move(): return lax.ppermute(value, AXES, permutation(target))  53.6 us
    ppermute x58, waiting for transfers between devices, move(): return lax.ppermute(value, AXES, permutation(target))  51.4 us
    pallas_call x3, Pallas kernels, attn_bwd(): pl.pallas_call(attn_bwd_kernel, grid_spec=pltpu.PrefetchScalarGridSpec(nu...  28.6 us
    pallas_call x3, Pallas kernels, attn_fwd(): pl.pallas_call(attn_fwd_kernel, grid_spec=pltpu.PrefetchScalarGridSpec(nu...  22.8 us
    pallas_call x2, Pallas kernels, grad_call(): pl.pallas_call(kernel, grid_spec=pltpu.PrefetchScalarGridSpec(num_scalar_...  13.6 us
    pallas_call x3, Pallas kernels, add_wide(): pl.pallas_call(add_kernel, grid=(second,), in_specs=[both, both], out_spe...  10.3 us
    pallas_call x1, Pallas kernels, ig(): pl.pallas_call(ig_fetch_kernel if fetched else ig_plain_kernel, grid_spec...  10.1 us
  transfers between devices with their start and end apart: 58, of which 16 were waited for; matrix products, arithmetic and copies ran while one was open for 2% of the time, Pallas kernels for 34%

profile of v1, /device:TPU:0, one launch (start us, length us, event | category | flops | bytes accessed | tf_op | source)
XLA Modules:
  0.0 284.1 jit_solution(13682066992994949621)
XLA Ops:
  4.1 5.1 %collective-permute-start.2 = (bf16[48,1280]{1,0:T(8,128)(2,1)}, bf16[48,1280]{1,0:T(8,128)(2,1)S(1)}, u32[]{:S(2)}, u32[]{:S(2)}) collective-permute-start(bf16[48,1280]{1,0:T(8,128)(2,1)} %get-tuple-element.150), channel_id=1, source_target_pairs={{0,24},{1,25},{2,26},{3,27},{4,28},{5,29},{6,30},{7,31},{8,0},{9,1... | collective-permute-start | bytes 368648 | tf_op jit(solution)/shard_map/ppermute | solution.py:73
  13.2 6.8 %collective-permute-done.1 = bf16[48,1280]{1,0:T(8,128)(2,1)S(1)} collective-permute-done((bf16[48,1280]{1,0:T(8,128)(2,1)}, bf16[48,1280]{1,0:T(8,128)(2,1)S(1)}, u32[]{:S(2)}, u32[]{:S(2)}) %collective-permute-start.1) | collective-permute-done | bytes 122912 | tf_op jit(solution)/shard_map/ppermute | solution.py:73
  29.4 11.3 %collective-permute-done.6 = bf16[48,1920]{1,0:T(8,128)(2,1)S(1)} collective-permute-done((bf16[48,1920]{1,0:T(8,128)(2,1)S(1)}, bf16[48,1920]{1,0:T(8,128)(2,1)S(1)}, u32[]{:S(2)}, u32[]{:S(2)}) %collective-permute-start.6) | collective-permute-done | bytes 184352 | tf_op jit(solution)/shard_map/ppermute | solution.py:73
  42.0 7.7 %collective-permute-done.8.refs_3_.refs_6_ = bf16[4,48,1280]{2,1,0:T(8,128)(2,1)S(1)} collective-permute-done((bf16[4,48,1280]{2,1,0:T(8,128)(2,1)S(1)}, bf16[4,48,1280]{2,1,0:T(8,128)(2,1)S(1)}, u32[]{:S(2)}, u32[]{:S(2)}) %collective-permute-start.8) | collective-permute-done | bytes 491552 | tf_op jit(solution)/shard_map/ppermute | solution.py:73
  53.4 9.3 %qkv_fetch.1 = (bf16[1024,768]{1,0:T(8,128)(2,1)}, bf16[1024,768]{1,0:T(8,128)(2,1)}, bf16[1024,768]{1,0:T(8,128)(2,1)}, f32[1,1536]{1,0:T(1,128)}, f32[1,768]{1...) custom-call(s32[4]{0:T(128)} %pad_add_fusion.pos, ...), custom_call_target="tpu_custom_call" | custom-call | flops 11500000256 | bytes 10000000 | tf_op jit(solution)/shard_map/qkv_fetch/pallas_call | solution.py:488
  65.3 7.6 %attn_fwd.3 = (bf16[1024,256]{1,0:T(8,128)(2,1)}, f32[2,2,2,512]{3,2,1,0:T(2,128)}) custom-call(s32[2]{0:T(128)} %cnt.11, bf16[1024,768]{1,0:T(8,128)(2,1)} %get-tuple-element.171.q_ref.k_ref.v_ref, bf16[1024,768]{1,0:T(8,128)(2,1)} %get-tuple-element.171.q_ref.k_ref.v_ref, bf16[1024,768]{1,0:T(8,128)(2,1)} %get-tuple-element.171.q_ref.k_ref.v_ref), custom_call_target="tpu_custom_call" | custom-call | flops 8049999872 | bytes 7000000 | tf_op jit(solution)/shard_map/attn_fwd/pallas_call | solution.py:559
  73.6 7.6 %attn_fwd.4 = (bf16[1024,256]{1,0:T(8,128)(2,1)}, f32[2,2,2,512]{3,2,1,0:T(2,128)}) custom-call(s32[2]{0:T(128)} %cnt.11, bf16[1024,768]{1,0:T(8,128)(2,1)} %get-tuple-element.214.q_ref.k_ref.v_ref, bf16[1024,768]{1,0:T(8,128)(2,1)} %get-tuple-element.214.q_ref.k_ref.v_ref, bf16[1024,768]{1,0:T(8,128)(2,1)} %get-tuple-element.214.q_ref.k_ref.v_ref), custom_call_target="tpu_custom_call" | custom-call | flops 8049999872 | bytes 7000000 | tf_op jit(solution)/shard_map/attn_fwd/pallas_call | solution.py:559
  86.1 7.6 %attn_fwd.5 = (bf16[1024,256]{1,0:T(8,128)(2,1)}, f32[2,2,2,512]{3,2,1,0:T(2,128)}) custom-call(s32[2]{0:T(128)} %cnt.11, bf16[1024,768]{1,0:T(8,128)(2,1)} %get-tuple-element.225.q_ref.k_ref.v_ref, bf16[1024,768]{1,0:T(8,128)(2,1)} %get-tuple-element.225.q_ref.k_ref.v_ref, bf16[1024,768]{1,0:T(8,128)(2,1)} %get-tuple-element.225.q_ref.k_ref.v_ref), custom_call_target="tpu_custom_call" | custom-call | flops 8049999872 | bytes 7000000 | tf_op jit(solution)/shard_map/attn_fwd/pallas_call | solution.py:559
  94.3 3.3 %collective-permute-done.22.refs_16_ = bf16[4,192,384]{2,1,0:T(8,128)(2,1)} collective-permute-done((bf16[4,192,384]{2,1,0:T(8,128)(2,1)}, bf16[4,192,384]{2,1,0:T(8,128)(2,1)}, u32[]{:S(2)}, u32[]{:S(2)}) %collective-permute-start.22) | collective-permute-done | bytes 589856 | tf_op jit(solution)/shard_map/ppermute | solution.py:73
  98.2 3.2 %collective-permute-done.28.refs_19_ = bf16[4,192,384]{2,1,0:T(8,128)(2,1)S(1)} collective-permute-done((bf16[4,192,384]{2,1,0:T(8,128)(2,1)}, bf16[4,192,384]{2,1,0:T(8,128)(2,1)S(1)}, u32[]{:S(2)}, u32[]{:S(2)}) %collective-permute-start.28) | collective-permute-done | bytes 589856 | tf_op jit(solution)/shard_map/ppermute | solution.py:73
  102.7 61.1 %main.1 = (bf16[1024,768]{1,0:T(8,128)(2,1)}, f32[1024,768]{1,0:T(8,128)}, bf16[1024,768]{1,0:T(8,128)(2,1)}, f32[1,768]{1,0:T(1,128)}, f32[1,768]{1,0:T(1,128)}...) custom-call(s32[4]{0:T(128)} %pad_add_fusion.pos, ...), custom_call_target="tpu_custom_call" | custom-call | flops 66700001280 | bytes 58000000 | tf_op jit(solution)/shard_map/main/pallas_call | solution.py:733
  164.4 9.5 %attn_bwd.3 = (bf16[1024,768]{1,0:T(8,128)(2,1)}, f32[1,256]{1,0:T(1,128)}, f32[1,256]{1,0:T(1,128)}) custom-call(s32[2]{0:T(128)} %cnt.11, bf16[1024,768]{1,0:T(8,128)(2,1)} %get-tuple-element.171.q_ref.k_ref.v_ref, bf16[1024,768]{1,0:T(8,128)(2,1)} %get-tuple-element.171.q_ref.k_ref.v_ref, bf16[1024,768]{1,0:T(8,128)(2,1)} %get-tuple-element.171.q_ref.k_ref.v_ref, ...), custom_call_target="tpu_custom_call" | custom-call | flops 10350000128 | bytes 9000000 | tf_op jit(solution)/shard_map/attn_bwd/pallas_call | solution.py:619
  175.3 3.6 %add_wide.3 = (bf16[2,4,192,384]{3,2,1,0:T(8,128)(2,1)}, bf16[2,4,192,384]{3,2,1,0:T(8,128)(2,1)}) custom-call(bf16[2,2,4,192,384]{4,3,2,1,0:T(8,128)(2,1)} %get-tuple-element.207.keep, bf16[2,2,4,192,384]{4,3,2,1,0:T(8,128)(2,1)} %copy-done.16), custom_call_target="tpu_custom_call" | custom-call | flops 4600000000 | bytes 4000000 | tf_op jit(solution)/shard_map/add_wide/pallas_call | solution.py:108
  179.5 4.0 %add_wide.4 = (bf16[2,4,48,1920]{3,2,1,0:T(8,128)(2,1)}, bf16[2,4,48,1920]{3,2,1,0:T(8,128)(2,1)}) custom-call(bf16[2,2,4,48,1920]{4,3,2,1,0:T(8,128)(2,1)} %get-tuple-element.210.keep, bf16[2,2,4,48,1920]{4,3,2,1,0:T(8,128)(2,1)} %collective-permute-done.30.got), custom_call_target="tpu_custom_call" | custom-call | flops 4600000000 | bytes 4000000 | tf_op jit(solution)/shard_map/add_wide/pallas_call | solution.py:108
  185.0 9.6 %attn_bwd.4 = (bf16[1024,768]{1,0:T(8,128)(2,1)}, f32[1,256]{1,0:T(1,128)}, f32[1,256]{1,0:T(1,128)}) custom-call(s32[2]{0:T(128)} %cnt.11, bf16[1024,768]{1,0:T(8,128)(2,1)} %get-tuple-element.214.q_ref.k_ref.v_ref, bf16[1024,768]{1,0:T(8,128)(2,1)} %get-tuple-element.214.q_ref.k_ref.v_ref, bf16[1024,768]{1,0:T(8,128)(2,1)} %get-tuple-element.214.q_ref.k_ref.v_ref, ...), custom_call_target="tpu_custom_call" | custom-call | flops 10350000128 | bytes 9000000 | tf_op jit(solution)/shard_map/attn_bwd/pallas_call | solution.py:619
  197.0 7.3 %grad_in.1 = (bf16[2,2,4,48,768]{4,3,2,1,0:T(8,128)(2,1)}, bf16[2,2,4,48,768]{4,3,2,1,0:T(8,128)(2,1)}) custom-call(s32[4]{0:T(128)} %pad_add_fusion.pos, bf16[1024,768]{1,0:T(8,128)(2,1)} %bitcast.107, bf16[1024,768]{1,0:T(8,128)(2,1)} %get-tuple-element.221.refs_0_, bf16[1024,768]{1,0:T(8,128)(2,1)} %get-tuple-element.222.refs_1_), custom_call_target="tpu_custom_call" | custom-call | flops 5750000128 | bytes 5000000 | tf_op jit(solution)/shard_map/grad_in/pallas_call | solution.py:358
  204.3 9.5 %attn_bwd.5 = (bf16[1024,768]{1,0:T(8,128)(2,1)}, f32[1,256]{1,0:T(1,128)}, f32[1,256]{1,0:T(1,128)}) custom-call(s32[2]{0:T(128)} %cnt.11, bf16[1024,768]{1,0:T(8,128)(2,1)} %get-tuple-element.225.q_ref.k_ref.v_ref, bf16[1024,768]{1,0:T(8,128)(2,1)} %get-tuple-element.225.q_ref.k_ref.v_ref, bf16[1024,768]{1,0:T(8,128)(2,1)} %get-tuple-element.225.q_ref.k_ref.v_ref, ...), custom_call_target="tpu_custom_call" | custom-call | flops 10350000128 | bytes 9000000 | tf_op jit(solution)/shard_map/attn_bwd/pallas_call | solution.py:619
  214.0 3.3 %collective-permute-start.41 = (bf16[192,384]{1,0:T(8,128)(2,1)S(1)}, bf16[192,384]{1,0:T(8,128)(2,1)S(1)}, u32[]{:S(2)}, u32[]{:S(2)}) collective-permute-start(bf16[192,384]{1,0:T(8,128)(2,1)S(1)} %get-tuple-element.303), channel_id=1, source_target_pairs={{0,24},{1,25},{2,26},{3,27},{4,28},{5,29},{6,30},{7,31},{8,0},{9,1... | collective-permute-start | bytes 442376 | tf_op jit(solution)/shard_map/ppermute | solution.py:73
  223.5 6.4 %grad_last.1 = (bf16[2,2,4,48,512]{4,3,2,1,0:T(8,128)(2,1)}, bf16[2,2,4,48,512]{4,3,2,1,0:T(8,128)(2,1)}) custom-call(s32[4]{0:T(128)} %pad_add_fusion.pos, bf16[1024,768]{1,0:T(8,128)(2,1)} %bitcast.108, bf16[1024,768]{1,0:T(8,128)(2,1)} %get-tuple-element.237.part.refs_2_, f32[1,256]{1,0:T(1,128)} %get-tuple-element.205.refs_0_, ...), custom_call_target="tpu_custom_call" | custom-call | flops 4600000000 | bytes 4000000 | tf_op jit(solution)/shard_map/grad_last/pallas_call | solution.py:358
  232.4 3.7 %collective-permute-done.38 = bf16[4,48,1920]{2,1,0:T(8,128)(2,1)S(1)} collective-permute-done((bf16[4,48,1920]{2,1,0:T(8,128)(2,1)S(1)}, bf16[4,48,1920]{2,1,0:T(8,128)(2,1)S(1)}, u32[]{:S(2)}, u32[]{:S(2)}) %collective-permute-start.38) | collective-permute-done | bytes 737312 | tf_op jit(solution)/shard_map/ppermute | solution.py:73
  237.1 3.6 %collective-permute-start.44 = (bf16[48,1920]{1,0:T(8,128)(2,1)}, bf16[48,1920]{1,0:T(8,128)(2,1)S(1)}, u32[]{:S(2)}, u32[]{:S(2)}) collective-permute-start(bf16[48,1920]{1,0:T(8,128)(2,1)} %get-tuple-element.296), channel_id=1, source_target_pairs={{0,24},{1,25},{2,26},{3,27},{4,28},{5,29},{6,30},{7,31},{8,0},{9,1... | collective-permute-start | bytes 552968 | tf_op jit(solution)/shard_map/ppermute | solution.py:73
  244.6 10.1 %ig.1 = bf16[1024,768]{1,0:T(8,128)(2,1)} custom-call(s32[4]{0:T(128)} %pad_add_fusion.pos, f32[1024,768]{1,0:T(8,128)} %get-tuple-element.255.gf, bf16[1024,768]{1,0:T(8,128)(2,1)} %get-tuple-element.221.refs_0_, bf16[1024,768]{1,0:T(8,128)(2,1)} %get-tuple-element.222.refs_1_, bf16[1024,768]{1,0:T(8,128)(2,1)} %get-tuple-element.237.part.refs_2_, ...), custom_call_target="tpu_custom_call" | custom-call | flops 11500000256 | bytes 10000000 | tf_op jit(solution)/shard_map/ig/pallas_call | solution.py:856
  256.2 3.6 %collective-permute-start.48 = (bf16[48,768]{1,0:T(8,128)(2,1)S(1)}, bf16[48,768]{1,0:T(8,128)(2,1)S(1)}, u32[]{:S(2)}, u32[]{:S(2)}) collective-permute-start(bf16[48,768]{1,0:T(8,128)(2,1)S(1)} %get-tuple-element.314), channel_id=1, source_target_pairs={{0,24},{1,25},{2,26},{3,27},{4,28},{5,29},{6,30},{7,31},{8,0},{9,1... | collective-permute-start | bytes 221192 | tf_op jit(solution)/shard_map/ppermute | solution.py:73
  262.0 3.6 %collective-permute-done.47 = bf16[48,768]{1,0:T(8,128)(2,1)S(1)} collective-permute-done((bf16[48,768]{1,0:T(8,128)(2,1)S(1)}, bf16[48,768]{1,0:T(8,128)(2,1)S(1)}, u32[]{:S(2)}, u32[]{:S(2)}) %collective-permute-start.47) | collective-permute-done | bytes 73760 | tf_op jit(solution)/shard_map/ppermute | solution.py:73
  (205 shorter events, 74.2 us)
Async XLA Ops:
  21.0 19.7 %collective-permute-start.4 = (bf16[4,48,1280]{2,1,0:T(8,128)(2,1)S(1)}, bf16[4,48,1280]{2,1,0:T(8,128)(2,1)S(1)}, u32[]{:S(2)}, u32[]{:S(2)}) collective-permute-start(bf16[4,48,1280]{2,1,0:T(8,128)(2,1)S(1)} %pad_maximum_fusion.2.refs_0_.refs_3_), channel_id=1, source_target_pairs={{0,4},{1,5},{2,3},{3,2},{4,0},{5,1},{6,7},{7,6},{8,12},{9,13},{10,... | collective-permute-start | bytes 1474568 | tf_op jit(solution)/shard_map/ppermute | solution.py:73
  24.3 16.4 %collective-permute-start.6 = (bf16[48,1920]{1,0:T(8,128)(2,1)S(1)}, bf16[48,1920]{1,0:T(8,128)(2,1)S(1)}, u32[]{:S(2)}, u32[]{:S(2)}) collective-permute-start(bf16[48,1920]{1,0:T(8,128)(2,1)S(1)} %copy-done.10), channel_id=1, source_target_pairs={{0,16},{1,17},{2,18},{3,19},{4,20},{5,21},{6,22},{7,23},{8,24},{9,... | collective-permute-start | bytes 552968 | tf_op jit(solution)/shard_map/ppermute | solution.py:73
  25.2 15.6 %collective-permute-start.5 = (bf16[48,1920]{1,0:T(8,128)(2,1)S(1)}, bf16[48,1920]{1,0:T(8,128)(2,1)S(1)}, u32[]{:S(2)}, u32[]{:S(2)}) collective-permute-start(bf16[48,1920]{1,0:T(8,128)(2,1)S(1)} %copy-done.10), channel_id=1, source_target_pairs={{0,8},{1,9},{2,10},{3,11},{4,12},{5,13},{6,14},{7,15},{8,16},{9,17... | collective-permute-start | bytes 552968 | tf_op jit(solution)/shard_map/ppermute | solution.py:73
  27.2 14.7 %collective-permute-start.3 = (bf16[4,48,1280]{2,1,0:T(8,128)(2,1)S(1)}, bf16[4,48,1280]{2,1,0:T(8,128)(2,1)S(1)}, u32[]{:S(2)}, u32[]{:S(2)}) collective-permute-start(bf16[4,48,1280]{2,1,0:T(8,128)(2,1)S(1)} %pad_maximum_fusion.2.refs_0_.refs_3_), channel_id=1, source_target_pairs={{0,1},{1,0},{2,6},{3,7},{4,5},{5,4},{6,2},{7,3},{8,9},{9,8},{10,14... | collective-permute-start | bytes 1474568 | tf_op jit(solution)/shard_map/ppermute | solution.py:73
  41.4 21.3 %collective-permute-start.15 = (bf16[192,384]{1,0:T(8,128)(2,1)S(1)}, bf16[192,384]{1,0:T(8,128)(2,1)S(1)}, u32[]{:S(2)}, u32[]{:S(2)}) collective-permute-start(bf16[192,384]{1,0:T(8,128)(2,1)S(1)} %copy-done.12), channel_id=1, source_target_pairs={{0,24},{1,25},{2,26},{3,27},{4,28},{5,29},{6,30},{7,31},{8,0},{9,1... | collective-permute-start | bytes 442376 | tf_op jit(solution)/shard_map/ppermute | solution.py:73
  51.2 30.0 %collective-permute-start.20 = (bf16[4,48,1920]{2,1,0:T(8,128)(2,1)S(1)}, bf16[4,48,1920]{2,1,0:T(8,128)(2,1)S(1)}, u32[]{:S(2)}, u32[]{:S(2)}) collective-permute-start(bf16[4,48,1920]{2,1,0:T(8,128)(2,1)S(1)} %pad_maximum_fusion.refs_5_), channel_id=1, source_target_pairs={{0,1},{1,0},{2,6},{3,7},{4,5},{5,4},{6,2},{7,3},{8,9},{9,8},{10,14... | collective-permute-start | bytes 2211848 | tf_op jit(solution)/shard_map/ppermute | solution.py:73
  51.9 21.0 %collective-permute-start.16 = (bf16[4,48,1920]{2,1,0:T(8,128)(2,1)S(1)}, bf16[4,48,1920]{2,1,0:T(8,128)(2,1)S(1)}, u32[]{:S(2)}, u32[]{:S(2)}) collective-permute-start(bf16[4,48,1920]{2,1,0:T(8,128)(2,1)S(1)} %pad_maximum_fusion.refs_5_), channel_id=1, source_target_pairs={{0,4},{1,5},{2,3},{3,2},{4,0},{5,1},{6,7},{7,6},{8,12},{9,13},{10,... | collective-permute-start | bytes 2211848 | tf_op jit(solution)/shard_map/ppermute | solution.py:73
  63.0 20.2 %collective-permute-start.18 = (bf16[4,192,384]{2,1,0:T(8,128)(2,1)S(1)}, bf16[4,192,384]{2,1,0:T(8,128)(2,1)}, u32[]{:S(2)}, u32[]{:S(2)}) collective-permute-start(bf16[4,192,384]{2,1,0:T(8,128)(2,1)S(1)} %pad_maximum_fusion.1.refs_13_), channel_id=1, source_target_pairs={{0,1},{1,0},{2,6},{3,7},{4,5},{5,4},{6,2},{7,3},{8,9},{9,8},{10,14... | collective-permute-start | bytes 1769480 | tf_op jit(solution)/shard_map/ppermute | solution.py:73
  64.6 19.5 %collective-permute-start.17 = (bf16[4,192,384]{2,1,0:T(8,128)(2,1)S(1)}, bf16[4,192,384]{2,1,0:T(8,128)(2,1)}, u32[]{:S(2)}, u32[]{:S(2)}) collective-permute-start(bf16[4,192,384]{2,1,0:T(8,128)(2,1)S(1)} %pad_maximum_fusion.1.refs_13_), channel_id=1, source_target_pairs={{0,4},{1,5},{2,3},{3,2},{4,0},{5,1},{6,7},{7,6},{8,12},{9,13},{10,... | collective-permute-start | bytes 1769480 | tf_op jit(solution)/shard_map/ppermute | solution.py:73
  73.0 20.8 %collective-permute-start.21 = (bf16[4,48,1920]{2,1,0:T(8,128)(2,1)S(1)}, bf16[4,48,1920]{2,1,0:T(8,128)(2,1)}, u32[]{:S(2)}, u32[]{:S(2)}) collective-permute-start(bf16[4,48,1920]{2,1,0:T(8,128)(2,1)S(1)} %collective-permute-done.16.refs_7_), channel_id=1, source_target_pairs={{0,1},{1,0},{2,6},{3,7},{4,5},{5,4},{6,2},{7,3},{8,9},{9,8},{10,14... | collective-permute-start | bytes 2211848 | tf_op jit(solution)/shard_map/ppermute | solution.py:73
  84.1 13.5 %collective-permute-start.22 = (bf16[4,192,384]{2,1,0:T(8,128)(2,1)}, bf16[4,192,384]{2,1,0:T(8,128)(2,1)}, u32[]{:S(2)}, u32[]{:S(2)}) collective-permute-start(bf16[4,192,384]{2,1,0:T(8,128)(2,1)} %collective-permute-done.17.refs_15_), channel_id=1, source_target_pairs={{0,1},{1,0},{2,6},{3,7},{4,5},{5,4},{6,2},{7,3},{8,9},{9,8},{10,14... | collective-permute-start | bytes 1769480 | tf_op jit(solution)/shard_map/ppermute | solution.py:73
  86.1 15.3 %collective-permute-start.23 = (bf16[4,48,1920]{2,1,0:T(8,128)(2,1)S(1)}, bf16[4,48,1920]{2,1,0:T(8,128)(2,1)S(1)}, u32[]{:S(2)}, u32[]{:S(2)}) collective-permute-start(bf16[4,48,1920]{2,1,0:T(8,128)(2,1)S(1)} %collective-permute-done.20.refs_6_), channel_id=1, source_target_pairs={{0,2},{1,3},{2,0},{3,1},{4,6},{5,7},{6,4},{7,5},{8,10},{9,11},{10,... | collective-permute-start | bytes 2211848 | tf_op jit(solution)/shard_map/ppermute | solution.py:73
  163.8 15.6 %collective-permute-start.30 = (bf16[2,2,4,48,1920]{4,3,2,1,0:T(8,128)(2,1)}, bf16[2,2,4,48,1920]{4,3,2,1,0:T(8,128)(2,1)}, u32[]{:S(2)}, u32[]{:S(2)}) collective-permute-start(bf16[2,2,4,48,1920]{4,3,2,1,0:T(8,128)(2,1)} %get-tuple-element.202), channel_id=1, source_target_pairs={{0,2},{1,3},{2,0},{3,1},{4,6},{5,7},{6,4},{7,5},{8,10},{9,11},{10,... | collective-permute-start | bytes 8847368 | tf_op jit(solution)/shard_map/ppermute | solution.py:73
  178.9 16.4 %collective-permute-start.32 = (bf16[2,4,192,384]{3,2,1,0:T(8,128)(2,1)}, bf16[2,4,192,384]{3,2,1,0:T(8,128)(2,1)S(1)}, u32[]{:S(2)}, u32[]{:S(2)}) collective-permute-start(bf16[2,4,192,384]{3,2,1,0:T(8,128)(2,1)} %get-tuple-element.209), channel_id=1, source_target_pairs={{0,1},{1,0},{2,6},{3,7},{4,5},{5,4},{6,2},{7,3},{8,9},{9,8},{10,14... | collective-permute-start | bytes 3538952 | tf_op jit(solution)/shard_map/ppermute | solution.py:73
  183.5 34.6 %collective-permute-start.34 = (bf16[2,4,48,1920]{3,2,1,0:T(8,128)(2,1)}, bf16[2,4,48,1920]{3,2,1,0:T(8,128)(2,1)S(1)}, u32[]{:S(2)}, u32[]{:S(2)}) collective-permute-start(bf16[2,4,48,1920]{3,2,1,0:T(8,128)(2,1)} %get-tuple-element.212), channel_id=1, source_target_pairs={{0,1},{1,0},{2,6},{3,7},{4,5},{5,4},{6,2},{7,3},{8,9},{9,8},{10,14... | collective-permute-start | bytes 4423688 | tf_op jit(solution)/shard_map/ppermute | solution.py:73
  196.0 17.8 %collective-permute-start.35 = (bf16[4,192,384]{2,1,0:T(8,128)(2,1)S(1)}, bf16[4,192,384]{2,1,0:T(8,128)(2,1)S(1)}, u32[]{:S(2)}, u32[]{:S(2)}) collective-permute-start(bf16[4,192,384]{2,1,0:T(8,128)(2,1)S(1)} %get-tuple-element.289), channel_id=1, source_target_pairs={{0,4},{1,5},{2,3},{3,2},{4,0},{5,1},{6,7},{7,6},{8,12},{9,13},{10,... | collective-permute-start | bytes 1769480 | tf_op jit(solution)/shard_map/ppermute | solution.py:73
  204.3 15.9 %collective-permute-start.33 = (bf16[2,2,4,48,768]{4,3,2,1,0:T(8,128)(2,1)}, bf16[2,2,4,48,768]{4,3,2,1,0:T(8,128)(2,1)}, u32[]{:S(2)}, u32[]{:S(2)}) collective-permute-start(bf16[2,2,4,48,768]{4,3,2,1,0:T(8,128)(2,1)} %get-tuple-element.224), channel_id=1, source_target_pairs={{0,2},{1,3},{2,0},{3,1},{4,6},{5,7},{6,4},{7,5},{8,10},{9,11},{10,... | collective-permute-start | bytes 3538952 | tf_op jit(solution)/shard_map/ppermute | solution.py:73
  214.0 17.2 %collective-permute-start.41 = (bf16[192,384]{1,0:T(8,128)(2,1)S(1)}, bf16[192,384]{1,0:T(8,128)(2,1)S(1)}, u32[]{:S(2)}, u32[]{:S(2)}) collective-permute-start(bf16[192,384]{1,0:T(8,128)(2,1)S(1)} %get-tuple-element.303), channel_id=1, source_target_pairs={{0,24},{1,25},{2,26},{3,27},{4,28},{5,29},{6,30},{7,31},{8,0},{9,1... | collective-permute-start | bytes 442376 | tf_op jit(solution)/shard_map/ppermute | solution.py:73
  217.3 14.1 %collective-permute-start.40 = (bf16[192,384]{1,0:T(8,128)(2,1)S(1)}, bf16[192,384]{1,0:T(8,128)(2,1)S(1)}, u32[]{:S(2)}, u32[]{:S(2)}) collective-permute-start(bf16[192,384]{1,0:T(8,128)(2,1)S(1)} %get-tuple-element.304), channel_id=1, source_target_pairs={{0,16},{1,17},{2,18},{3,19},{4,20},{5,21},{6,22},{7,23},{8,24},{9,... | collective-permute-start | bytes 442376 | tf_op jit(solution)/shard_map/ppermute | solution.py:73
  217.7 13.7 %collective-permute-start.39 = (bf16[192,384]{1,0:T(8,128)(2,1)S(1)}, bf16[192,384]{1,0:T(8,128)(2,1)}, u32[]{:S(2)}, u32[]{:S(2)}) collective-permute-start(bf16[192,384]{1,0:T(8,128)(2,1)S(1)} %get-tuple-element.305), channel_id=1, source_target_pairs={{0,8},{1,9},{2,10},{3,11},{4,12},{5,13},{6,14},{7,15},{8,16},{9,17... | collective-permute-start | bytes 442376 | tf_op jit(solution)/shard_map/ppermute | solution.py:73
  218.8 17.3 %collective-permute-start.38 = (bf16[4,48,1920]{2,1,0:T(8,128)(2,1)S(1)}, bf16[4,48,1920]{2,1,0:T(8,128)(2,1)S(1)}, u32[]{:S(2)}, u32[]{:S(2)}) collective-permute-start(bf16[4,48,1920]{2,1,0:T(8,128)(2,1)S(1)} %get-tuple-element.287), channel_id=1, source_target_pairs={{0,4},{1,5},{2,3},{3,2},{4,0},{5,1},{6,7},{7,6},{8,12},{9,13},{10,... | collective-permute-start | bytes 2211848 | tf_op jit(solution)/shard_map/ppermute | solution.py:73
  222.9 19.2 %collective-permute-start.36 = (bf16[2,4,48,768]{3,2,1,0:T(8,128)(2,1)}, bf16[2,4,48,768]{3,2,1,0:T(8,128)(2,1)S(1)}, u32[]{:S(2)}, u32[]{:S(2)}) collective-permute-start(bf16[2,4,48,768]{3,2,1,0:T(8,128)(2,1)} %get-tuple-element.236), channel_id=1, source_target_pairs={{0,1},{1,0},{2,6},{3,7},{4,5},{5,4},{6,2},{7,3},{8,9},{9,8},{10,14... | collective-permute-start | bytes 1769480 | tf_op jit(solution)/shard_map/ppermute | solution.py:73
  237.1 17.7 %collective-permute-start.44 = (bf16[48,1920]{1,0:T(8,128)(2,1)}, bf16[48,1920]{1,0:T(8,128)(2,1)S(1)}, u32[]{:S(2)}, u32[]{:S(2)}) collective-permute-start(bf16[48,1920]{1,0:T(8,128)(2,1)} %get-tuple-element.296), channel_id=1, source_target_pairs={{0,24},{1,25},{2,26},{3,27},{4,28},{5,29},{6,30},{7,31},{8,0},{9,1... | collective-permute-start | bytes 552968 | tf_op jit(solution)/shard_map/ppermute | solution.py:73
  240.7 14.1 %collective-permute-start.43 = (bf16[48,1920]{1,0:T(8,128)(2,1)}, bf16[48,1920]{1,0:T(8,128)(2,1)S(1)}, u32[]{:S(2)}, u32[]{:S(2)}) collective-permute-start(bf16[48,1920]{1,0:T(8,128)(2,1)} %get-tuple-element.297), channel_id=1, source_target_pairs={{0,16},{1,17},{2,18},{3,19},{4,20},{5,21},{6,22},{7,23},{8,24},{9,... | collective-permute-start | bytes 552968 | tf_op jit(solution)/shard_map/ppermute | solution.py:73
  (65 other events, 579.4 us)

commit v2 on v1

--- a/solution.py
+++ b/solution.py
@@ -1,3 +1,4 @@
+import functools
 import math
 
 import jax
@@ -577,8 +578,11 @@
     )(counts, rows, rows, rows)
 
 
-def attn_bwd_kernel(cnt,q_ref,k_ref,v_ref,g_ref,o_ref,l_ref,d_ref,bq_ref,bv_ref):
-    p=pl.program_id(1)
+def attn_bwd_plain_kernel(*refs):
+    attn_bwd_kernel(pl.program_id(1), *refs)
+
+
+def attn_bwd_kernel(p,cnt,q_ref,k_ref,v_ref,g_ref,o_ref,l_ref,d_ref,bq_ref,bv_ref):
     q=q_ref[...];k=k_ref[...];v=v_ref[...];g=g_ref[...]
     lane=lax.broadcasted_iota(jnp.int32,q.shape,1)
     row=lax.broadcasted_iota(jnp.int32,q.shape,0)
@@ -617,7 +621,7 @@
     block = lambda o: pl.BlockSpec((length, 128), lambda h, p, c: (p, 3 * h + o))
     line = pl.BlockSpec((1, 128), lambda h, p, c: (0, h))
     return pl.pallas_call(
-        attn_bwd_kernel,
+        attn_bwd_plain_kernel,
         grid_spec=pltpu.PrefetchScalarGridSpec(
             num_scalar_prefetch=1,
             grid=(pairs, pages),
@@ -637,6 +641,113 @@
         cost_estimate=cost(4.5 * pairs),
         name="attn_bwd",
     )(counts, rows, rows, rows, grad, out, totals)
+
+
+def back_kernel(last, pos, cnt, q, k, v, g, o, l, x_all, prev_all, *refs):
+    more = refs[: 2 * (THIRDS - 1) + 7] if last else ()
+    d, bq, bv, keep, send, xs, prev, ds, held, *sems = refs[len(more) :]
+    step = pl.program_id(0)
+    pages = xs.shape[0] // q.shape[0]
+    work = ds.shape[1] // CW * pages
+    copies = [pltpu.make_async_copy(x_all, xs, sems[0])]
+    if not last:
+        copies.append(pltpu.make_async_copy(prev_all, prev, sems[1]))
+
+    @pl.when(step == 0)
+    def _():
+        for copy in copies:
+            copy.start()
+
+    @pl.when(step < work)
+    def _():
+        pair, page = step // pages, step % pages
+        rows = pl.ds(pl.multiple_of(page * q.shape[0], 16), q.shape[0])
+        here = ds.at[rows, pl.ds(pl.multiple_of(pair * CW, 128), CW)]
+        lane = pl.ds(pl.multiple_of(pair * 128, 128), 128)
+        attn_bwd_kernel(page, cnt, q, k, v, g, o, l, here, bq.at[:, lane], bv.at[:, lane])
+        d[...] = here[...]
+
+    @pl.when(step == work)
+    def _():
+        for copy in copies:
+            copy.wait()
+
+    if last:
+
+        @pl.when(step == work)
+        def _():
+            hold(held, dg(xs[...], ds[...], TN))
+            take = lambda ref: ref.at[:, :, :, :, pl.ds(0, CW)]
+            place_tile(pos, held, take(keep), take(send), 48, whole_line(pos))
+            half = THIRDS - 1
+            biases = (*more[:half], bq, *more[half : 2 * half], bv)
+            upb, outb, g1, s1, downb, g2, s2 = more[2 * half :]
+            groups = ((joined(biases), upb[...]), [r[...] for r in (outb, g1, s1, downb, g2, s2)])
+            for n in range(2):
+                held[n, :, :TINY] = tiny_rows(groups[n], FIELDS[n])
+            take = lambda ref: ref.at[:, :, :, :, pl.ds(CW, TINY)]
+            place_tile(pos, held.at[:, :, pl.ds(0, TINY)], take(keep), take(send), 48, whole_line(pos))
+
+    else:
+        for i, ref in enumerate((prev, ds)):
+
+            @pl.when(step == work + i)
+            def _(ref=ref):
+                hold(held, dg(xs[...], ref[...], TN))
+                place_tile(pos, held, keep, send, 48, whole_line(pos))
+
+
+def back_third(pos, counts, rows, grad, out, totals, pages, at, x, prev, vectors=None):
+    tokens, width = rows.shape
+    model = x.shape[1]
+    length, pairs = tokens // pages, width // CW
+    work = pairs * pages
+    last = vectors is not None
+    pair = lambda i: jnp.minimum(i, work - 1) // pages
+    page = lambda i: jnp.minimum(i, work - 1) % pages
+    part = lambda o: pl.BlockSpec((length, 128), lambda i, p, c: (page(i), 3 * pair(i) + o))
+    full = lambda a: pl.BlockSpec(a.shape, lambda i, p, c: (0, 0))
+    line = pl.BlockSpec((1, pairs * 128), lambda i, p, c: (0, 0))
+    any_space = pl.BlockSpec(memory_space=pl.ANY)
+    wide = CW + TINY if last else CW
+    grads = pl.BlockSpec((2, 2, LINE, 48, wide), lambda i, p, c: (0, 0, 0, 0, jnp.maximum(i - work, 0)))
+    shape = (2, 2, LINE, 48, wide if last else 2 * CW)
+    vectors = tuple(vectors or ())
+    return pl.pallas_call(
+        functools.partial(back_kernel, last),
+        grid_spec=pltpu.PrefetchScalarGridSpec(
+            num_scalar_prefetch=2,
+            grid=(work + (1 if last else 2),),
+            in_specs=[
+                part(0),
+                part(1),
+                part(2),
+                pl.BlockSpec((length, 128), lambda i, p, c: (page(i), pair(i) + at)),
+                pl.BlockSpec((length, 128), lambda i, p, c: (page(i), pair(i))),
+                pl.BlockSpec((1, 1, 2, length), lambda i, p, c: (page(i), pair(i), 0, 0)),
+                any_space,
+                any_space,
+            ]
+            + [full(a) for a in vectors],
+            out_specs=[pl.BlockSpec((length, CW), lambda i, p, c: (page(i), pair(i)))]
+            + [line] * 2
+            + [grads] * 2,
+            scratch_shapes=[
+                pltpu.VMEM((tokens, model), BF),
+                pltpu.VMEM((tokens, width), BF),
+                pltpu.VMEM((tokens, width), BF),
+                pltpu.VMEM((2, 16 * 48, CW), BF),
+                pltpu.SemaphoreType.DMA,
+                pltpu.SemaphoreType.DMA,
+            ],
+        ),
+        out_shape=[jax.ShapeDtypeStruct((tokens, width), BF)]
+        + [jax.ShapeDtypeStruct((1, pairs * 128), F32)] * 2
+        + [jax.ShapeDtypeStruct(shape, BF)] * 2,
+        compiler_params=params(),
+        cost_estimate=cost(13),
+        name="back_last" if last else "back_third",
+    )(pos, counts, rows, rows, rows, grad, out, totals, x, prev, *vectors)
 
 
 def norm(t):
@@ -966,23 +1077,24 @@
         first_d = move(go_d, to_first)
         go_u, stay_u = add_wide(*after((keep_u, core_u), go_d))
         first_u = move(go_u, to_first)
-        back(1, after(rows[1], go_u, stay_u))
+        *backward[1], keep_i, send_i = back_third(
+            pos, page_counts, after(rows[1], go_u, stay_u), grad_att, *forward[1], pages, pairs, x, backward[0][0]
+        )
         go_d, stay_d = add_core(*after((stay_d, first_d), backward[1]))
         second_d = move(go_d, to_second)
-        keep_i, send_i = grad_in(pos, x, after((backward[0][0], backward[1][0]), go_d, stay_d))
         core_i = move(send_i, to_core)
         back(2, after(rows[2], keep_i))
-        low_d = add_last(*after((stay_d, second_d), backward[2]))
-        line_d = move_line(low_d)
-        go_u, stay_u = add_core(*after((stay_u, first_u), low_d))
-        second_u = move(go_u, to_second)
         parts = tuple(b[0] for b in backward)
         vbq = [b[1] for b in backward]
         vbv = [b[2] for b in backward]
+        go_u, stay_u = add_core(*after((stay_u, first_u), backward[2]))
+        second_u = move(go_u, to_second)
         go_i, stay_i = add_wide(*after((keep_i, core_i), go_u, stay_u))
         first_i = move(go_i, to_first)
+        low_d = add_last(*after((stay_d, second_d), go_i))
+        line_d = move_line(low_d)
         keep_l, send_l = grad_last(
-            pos, x, after(parts[2], go_i, stay_i), (*vbq, *vbv, vub, vob, vg1, vs1, vdb, vg2, vs2)
+            pos, x, after(parts[2], go_i, stay_i, low_d), (*vbq, *vbv, vub, vob, vg1, vs1, vdb, vg2, vs2)
         )
         core_l = move(send_l, to_core)
         mine_d = add_line(low_d, after(line_d, keep_l))

time: 288 us -> 288 us (level)
  waiting for transfers between devices: 51.4 us -> 57.5 us
  starting transfers between devices: 53.6 us -> 50.1 us
  Pallas kernels: 164 us -> 161 us
    pallas_call x2 -> x1, Pallas kernels: 13.6 us -> 6.37 us  [grad_call(): pl.pallas_call(kernel, grid_spec=pltpu.PrefetchScalarGridSpec(num_scalar_...]
    ppermute x58, waiting for transfers between devices: 51.4 us -> 57.5 us  [move(): return lax.ppermute(value, AXES, permutation(target))]
    pallas_call x3, Pallas kernels: 28.6 us -> 32.8 us  [the longest x2 19.1 us: attn_bwd(): pl.pallas_call(attn_bwd_plain_kernel, grid_spec=pltpu.PrefetchScalarGridS...]
    ppermute x58, starting transfers between devices: 53.6 us -> 50.1 us  [move(): return lax.ppermute(value, AXES, permutation(target))]
  transfers between devices with their start and end apart: 58 -> 58, of which waited for: 16 -> 17; matrix products, arithmetic and copies ran while one was open for 2% -> 3% of each run, Pallas kernels for 34% -> 33%
where the time goes in v2:
time: 288 us; the launch traced here: 284 us
  Pallas kernels  161 us (56%)
  waiting for transfers between devices  57.5 us (20%)
  starting transfers between devices  50.1 us (17%)
  other arithmetic  8.99 us (3%)
  local copies, waits for them, and re-layouts  5.17 us (2%)
    pallas_call x1, Pallas kernels, main_fetch(): pl.pallas_call(main_fetch_kernel, grid_spec=pltpu.PrefetchScalarGridSpec(...  61.4 us
    ppermute x58, waiting for transfers between devices, move(): return lax.ppermute(value, AXES, permutation(target))  57.5 us
    ppermute x58, starting transfers between devices, move(): return lax.ppermute(value, AXES, permutation(target))  50.1 us
    pallas_call x3, Pallas kernels, attn_fwd(): pl.pallas_call(attn_fwd_kernel, grid_spec=pltpu.PrefetchScalarGridSpec(nu...  22.9 us
    pallas_call x2, Pallas kernels, attn_bwd(): pl.pallas_call(attn_bwd_plain_kernel, grid_spec=pltpu.PrefetchScalarGridS...  19.1 us
    pallas_call x1, Pallas kernels, back_third(): pl.pallas_call(functools.partial(back_kernel, last), grid_spec=pltpu.Pref...  13.7 us
    pallas_call x1, Pallas kernels, ig(): pl.pallas_call(ig_fetch_kernel if fetched else ig_plain_kernel, grid_spec...  10.1 us
    pallas_call x3, Pallas kernels, add_wide(): pl.pallas_call(add_kernel, grid=(second,), in_specs=[both, both], out_spe...  10.1 us
  transfers between devices with their start and end apart: 58, of which 17 were waited for; matrix products, arithmetic and copies ran while one was open for 3% of the time, Pallas kernels for 33%

profile of v2, /device:TPU:0, one launch (start us, length us, event | category | flops | bytes accessed | tf_op | source)
XLA Modules:
  0.0 284.3 jit_solution(11609454041425281617)
XLA Ops:
  4.0 5.1 %collective-permute-start.2 = (bf16[48,1280]{1,0:T(8,128)(2,1)}, bf16[48,1280]{1,0:T(8,128)(2,1)S(1)}, u32[]{:S(2)}, u32[]{:S(2)}) collective-permute-start(bf16[48,1280]{1,0:T(8,128)(2,1)} %get-tuple-element.148), channel_id=1, source_target_pairs={{0,24},{1,25},{2,26},{3,27},{4,28},{5,29},{6,30},{7,31},{8,0},{9,1... | collective-permute-start | bytes 368648 | tf_op jit(solution)/shard_map/ppermute | solution.py:74
  10.2 3.0 %collective-permute-done.2 = bf16[48,1280]{1,0:T(8,128)(2,1)S(1)} collective-permute-done((bf16[48,1280]{1,0:T(8,128)(2,1)}, bf16[48,1280]{1,0:T(8,128)(2,1)S(1)}, u32[]{:S(2)}, u32[]{:S(2)}) %collective-permute-start.2) | collective-permute-done | bytes 122912 | tf_op jit(solution)/shard_map/ppermute | solution.py:74
  13.2 6.8 %collective-permute-done.1 = bf16[48,1280]{1,0:T(8,128)(2,1)S(1)} collective-permute-done((bf16[48,1280]{1,0:T(8,128)(2,1)}, bf16[48,1280]{1,0:T(8,128)(2,1)S(1)}, u32[]{:S(2)}, u32[]{:S(2)}) %collective-permute-start.1) | collective-permute-done | bytes 122912 | tf_op jit(solution)/shard_map/ppermute | solution.py:74
  29.4 11.3 %collective-permute-done.6 = bf16[48,1920]{1,0:T(8,128)(2,1)S(1)} collective-permute-done((bf16[48,1920]{1,0:T(8,128)(2,1)S(1)}, bf16[48,1920]{1,0:T(8,128)(2,1)S(1)}, u32[]{:S(2)}, u32[]{:S(2)}) %collective-permute-start.6) | collective-permute-done | bytes 184352 | tf_op jit(solution)/shard_map/ppermute | solution.py:74
  41.9 7.7 %collective-permute-done.8.refs_3_.refs_6_ = bf16[4,48,1280]{2,1,0:T(8,128)(2,1)S(1)} collective-permute-done((bf16[4,48,1280]{2,1,0:T(8,128)(2,1)S(1)}, bf16[4,48,1280]{2,1,0:T(8,128)(2,1)S(1)}, u32[]{:S(2)}, u32[]{:S(2)}) %collective-permute-start.8) | collective-permute-done | bytes 491552 | tf_op jit(solution)/shard_map/ppermute | solution.py:74
  53.5 9.3 %qkv_fetch.1 = (bf16[1024,768]{1,0:T(8,128)(2,1)}, bf16[1024,768]{1,0:T(8,128)(2,1)}, bf16[1024,768]{1,0:T(8,128)(2,1)}, f32[1,1536]{1,0:T(1,128)}, f32[1,768]{1...) custom-call(s32[4]{0:T(128)} %pad_add_fusion.pos, ...), custom_call_target="tpu_custom_call" | custom-call | flops 11500000256 | bytes 10000000 | tf_op jit(solution)/shard_map/qkv_fetch/pallas_call | solution.py:489
  65.3 7.6 %attn_fwd.3 = (bf16[1024,256]{1,0:T(8,128)(2,1)}, f32[2,2,2,512]{3,2,1,0:T(2,128)}) custom-call(s32[2]{0:T(128)} %refs_0_.5, bf16[1024,768]{1,0:T(8,128)(2,1)} %get-tuple-element.169.q_ref.k_ref.v_ref.refs_1_.refs_2_.refs_3_, bf16[1024,768]{1,0:T(8,128)(2,1)} %get-tuple-element.169.q_ref.k_ref.v_ref.refs_1_.refs_2_.refs_3_, ...), custom_call_target="tpu_custom_call" | custom-call | flops 8049999872 | bytes 7000000 | tf_op jit(solution)/shard_map/attn_fwd/pallas_call | solution.py:560
  73.8 7.6 %attn_fwd.4 = (bf16[1024,256]{1,0:T(8,128)(2,1)}, f32[2,2,2,512]{3,2,1,0:T(2,128)}) custom-call(s32[2]{0:T(128)} %refs_0_.5, bf16[1024,768]{1,0:T(8,128)(2,1)} %get-tuple-element.212.q_ref.k_ref.v_ref.q.k.v, bf16[1024,768]{1,0:T(8,128)(2,1)} %get-tuple-element.212.q_ref.k_ref.v_ref.q.k.v, bf16[1024,768]{1,0:T(8,128)(2,1)} %get-tuple-element.212.q_ref.k_ref.v_ref.q.k.v), custom_call_target="tpu_custom_call" | custom-call | flops 8049999872 | bytes 7000000 | tf_op jit(solution)/shard_map/attn_fwd/pallas_call | solution.py:560
  86.1 7.6 %attn_fwd.5 = (bf16[1024,256]{1,0:T(8,128)(2,1)}, f32[2,2,2,512]{3,2,1,0:T(2,128)}) custom-call(s32[2]{0:T(128)} %refs_0_.5, bf16[1024,768]{1,0:T(8,128)(2,1)} %get-tuple-element.215.q_ref.k_ref.v_ref.refs_1_.refs_2_.refs_3_, bf16[1024,768]{1,0:T(8,128)(2,1)} %get-tuple-element.215.q_ref.k_ref.v_ref.refs_1_.refs_2_.refs_3_, ...), custom_call_target="tpu_custom_call" | custom-call | flops 8049999872 | bytes 7000000 | tf_op jit(solution)/shard_map/attn_fwd/pallas_call | solution.py:560
  94.3 3.3 %collective-permute-done.22.refs_16_ = bf16[4,192,384]{2,1,0:T(8,128)(2,1)} collective-permute-done((bf16[4,192,384]{2,1,0:T(8,128)(2,1)}, bf16[4,192,384]{2,1,0:T(8,128)(2,1)}, u32[]{:S(2)}, u32[]{:S(2)}) %collective-permute-start.22) | collective-permute-done | bytes 589856 | tf_op jit(solution)/shard_map/ppermute | solution.py:74
  98.2 3.2 %collective-permute-done.28.refs_19_ = bf16[4,192,384]{2,1,0:T(8,128)(2,1)S(1)} collective-permute-done((bf16[4,192,384]{2,1,0:T(8,128)(2,1)}, bf16[4,192,384]{2,1,0:T(8,128)(2,1)S(1)}, u32[]{:S(2)}, u32[]{:S(2)}) %collective-permute-start.28) | collective-permute-done | bytes 589856 | tf_op jit(solution)/shard_map/ppermute | solution.py:74
  102.7 61.4 %main.1 = (bf16[1024,768]{1,0:T(8,128)(2,1)}, f32[1024,768]{1,0:T(8,128)}, bf16[1024,768]{1,0:T(8,128)(2,1)}, f32[1,768]{1,0:T(1,128)}, f32[1,768]{1,0:T(1,128)}...) custom-call(s32[4]{0:T(128)} %pad_add_fusion.pos, ...), custom_call_target="tpu_custom_call" | custom-call | flops 66700001280 | bytes 58000000 | tf_op jit(solution)/shard_map/main/pallas_call | solution.py:844
  164.7 9.5 %attn_bwd.2 = (bf16[1024,768]{1,0:T(8,128)(2,1)}, f32[1,256]{1,0:T(1,128)}, f32[1,256]{1,0:T(1,128)}) custom-call(s32[2]{0:T(128)} %refs_0_.5, bf16[1024,768]{1,0:T(8,128)(2,1)} %get-tuple-element.169.q_ref.k_ref.v_ref.refs_1_.refs_2_.refs_3_, bf16[1024,768]{1,0:T(8,128)(2,1)} %get-tuple-element.169.q_ref.k_ref.v_ref.refs_1_.refs_2_.refs_3_, ...), custom_call_target="tpu_custom_call" | custom-call | flops 10350000128 | bytes 9000000 | tf_op jit(solution)/shard_map/attn_bwd/pallas_call | solution.py:623
  175.6 3.6 %add_wide.3 = (bf16[2,4,192,384]{3,2,1,0:T(8,128)(2,1)}, bf16[2,4,192,384]{3,2,1,0:T(8,128)(2,1)}) custom-call(bf16[2,2,4,192,384]{4,3,2,1,0:T(8,128)(2,1)} %get-tuple-element.205.keep, bf16[2,2,4,192,384]{4,3,2,1,0:T(8,128)(2,1)} %copy-done.16), custom_call_target="tpu_custom_call" | custom-call | flops 4600000000 | bytes 4000000 | tf_op jit(solution)/shard_map/add_wide/pallas_call | solution.py:109
  179.8 4.0 %add_wide.4 = (bf16[2,4,48,1920]{3,2,1,0:T(8,128)(2,1)}, bf16[2,4,48,1920]{3,2,1,0:T(8,128)(2,1)}) custom-call(bf16[2,2,4,48,1920]{4,3,2,1,0:T(8,128)(2,1)} %get-tuple-element.208.keep, bf16[2,2,4,48,1920]{4,3,2,1,0:T(8,128)(2,1)} %collective-permute-done.30.got), custom_call_target="tpu_custom_call" | custom-call | flops 4600000000 | bytes 4000000 | tf_op jit(solution)/shard_map/add_wide/pallas_call | solution.py:109
  185.2 13.7 %back_third.1 = (bf16[1024,768]{1,0:T(8,128)(2,1)}, f32[1,256]{1,0:T(1,128)}, f32[1,256]{1,0:T(1,128)}, bf16[2,2,4,48,768]{4,3,2,1,0:T(8,128)(2,1)}, bf16[2,2,4,48,768]{4,3,2,1,0:T(8,128)(2,1)}) custom-call(s32[4]{0:T(128)} %pad_add_fusion.pos, s32[2]{0:T(128)} %refs_0_.5, bf16[1024,768]{1,0:T(8,128)(2,1)} %get-tuple-element.212.q_ref.k_ref.v_ref.q.k.v, ...), custom_call_target="tpu_custom_call" | custom-call | flops 14949999616 | bytes 13000000 | tf_op jit(solution)/shard_map/back_third/pallas_call | solution.py:716
  199.0 9.6 %attn_bwd.3 = (bf16[1024,768]{1,0:T(8,128)(2,1)}, f32[1,256]{1,0:T(1,128)}, f32[1,256]{1,0:T(1,128)}) custom-call(s32[2]{0:T(128)} %refs_0_.5, bf16[1024,768]{1,0:T(8,128)(2,1)} %get-tuple-element.215.q_ref.k_ref.v_ref.refs_1_.refs_2_.refs_3_, bf16[1024,768]{1,0:T(8,128)(2,1)} %get-tuple-element.215.q_ref.k_ref.v_ref.refs_1_.refs_2_.refs_3_, ...), custom_call_target="tpu_custom_call" | custom-call | flops 10350000128 | bytes 9000000 | tf_op jit(solution)/shard_map/attn_bwd/pallas_call | solution.py:623
  216.2 5.1 %collective-permute-done.36 = bf16[4,192,384]{2,1,0:T(8,128)(2,1)} collective-permute-done((bf16[4,192,384]{2,1,0:T(8,128)(2,1)S(1)}, bf16[4,192,384]{2,1,0:T(8,128)(2,1)}, u32[]{:S(2)}, u32[]{:S(2)}) %collective-permute-start.36) | collective-permute-done | bytes 589856 | tf_op jit(solution)/shard_map/ppermute | solution.py:74
  222.6 3.7 %collective-permute-start.41 = (bf16[192,384]{1,0:T(8,128)(2,1)S(1)}, bf16[192,384]{1,0:T(8,128)(2,1)S(1)}, u32[]{:S(2)}, u32[]{:S(2)}) collective-permute-start(bf16[192,384]{1,0:T(8,128)(2,1)S(1)} %get-tuple-element.299), channel_id=1, source_target_pairs={{0,24},{1,25},{2,26},{3,27},{4,28},{5,29},{6,30},{7,31},{8,0},{9,1... | collective-permute-start | bytes 442376 | tf_op jit(solution)/shard_map/ppermute | solution.py:74
  227.1 6.4 %grad_last.1 = (bf16[2,2,4,48,512]{4,3,2,1,0:T(8,128)(2,1)}, bf16[2,2,4,48,512]{4,3,2,1,0:T(8,128)(2,1)}) custom-call(s32[4]{0:T(128)} %pad_add_fusion.pos, bf16[1024,768]{1,0:T(8,128)(2,1)} %bitcast.108, bf16[1024,768]{1,0:T(8,128)(2,1)} %get-tuple-element.233.part.refs_2_, f32[1,256]{1,0:T(1,128)} %get-tuple-element.203.refs_0_, ...), custom_call_target="tpu_custom_call" | custom-call | flops 4600000000 | bytes 4000000 | tf_op jit(solution)/shard_map/grad_last/pallas_call | solution.py:359
  245.7 10.1 %ig.1 = bf16[1024,768]{1,0:T(8,128)(2,1)} custom-call(s32[4]{0:T(128)} %pad_add_fusion.pos, f32[1024,768]{1,0:T(8,128)} %get-tuple-element.251.gf, bf16[1024,768]{1,0:T(8,128)(2,1)} %get-tuple-element.202.prev_all.refs_0_, bf16[1024,768]{1,0:T(8,128)(2,1)} %get-tuple-element.226.refs_1_, bf16[1024,768]{1,0:T(8,128)(2,1)} %get-tuple-element.233.part.refs_2_, ...), custom_call_target="tpu_custom_call" | custom-call | flops 11500000256 | bytes 10000000 | tf_op jit(solution)/shard_map/ig/pallas_call | solution.py:967
  263.8 3.9 %collective-permute-done.47 = bf16[48,768]{1,0:T(8,128)(2,1)S(1)} collective-permute-done((bf16[48,768]{1,0:T(8,128)(2,1)S(1)}, bf16[48,768]{1,0:T(8,128)(2,1)S(1)}, u32[]{:S(2)}, u32[]{:S(2)}) %collective-permute-start.47) | collective-permute-done | bytes 73760 | tf_op jit(solution)/shard_map/ppermute | solution.py:74
  276.7 3.2 %collective-permute-done.57.got_last = bf16[48,512]{1,0:T(8,128)(2,1)S(1)} collective-permute-done((bf16[48,512]{1,0:T(8,128)(2,1)S(1)}, bf16[48,512]{1,0:T(8,128)(2,1)S(1)}, u32[]{:S(2)}, u32[]{:S(2)}) %collective-permute-start.57) | collective-permute-done | bytes 49184 | tf_op jit(solution)/shard_map/ppermute | solution.py:74
  281.1 2.9 %finish.1 = (f32[48,768]{1,0:T(8,128)}, f32[48,3072]{1,0:T(8,128)}, f32[48,2304]{1,0:T(8,128)}, f32[1,96]{1,0:T(1,128)}, f32[1,48]{1,0:T(1,128)}, /*index=5*/f32...) custom-call(s32[4]{0:T(128)} %pad_add_fusion.pos, ...), custom_call_target="tpu_custom_call" | custom-call | tf_op jit(solution)/shard_map/finish/pallas_call | solution.py:428
  (204 shorter events, 73.3 us)
Async XLA Ops:
  21.0 19.7 %collective-permute-start.4 = (bf16[4,48,1280]{2,1,0:T(8,128)(2,1)S(1)}, bf16[4,48,1280]{2,1,0:T(8,128)(2,1)S(1)}, u32[]{:S(2)}, u32[]{:S(2)}) collective-permute-start(bf16[4,48,1280]{2,1,0:T(8,128)(2,1)S(1)} %pad_maximum_fusion.2.refs_0_.refs_3_), channel_id=1, source_target_pairs={{0,4},{1,5},{2,3},{3,2},{4,0},{5,1},{6,7},{7,6},{8,12},{9,13},{10,... | collective-permute-start | bytes 1474568 | tf_op jit(solution)/shard_map/ppermute | solution.py:74
  24.3 16.4 %collective-permute-start.6 = (bf16[48,1920]{1,0:T(8,128)(2,1)S(1)}, bf16[48,1920]{1,0:T(8,128)(2,1)S(1)}, u32[]{:S(2)}, u32[]{:S(2)}) collective-permute-start(bf16[48,1920]{1,0:T(8,128)(2,1)S(1)} %copy-done.10), channel_id=1, source_target_pairs={{0,16},{1,17},{2,18},{3,19},{4,20},{5,21},{6,22},{7,23},{8,24},{9,... | collective-permute-start | bytes 552968 | tf_op jit(solution)/shard_map/ppermute | solution.py:74
  25.1 15.6 %collective-permute-start.5 = (bf16[48,1920]{1,0:T(8,128)(2,1)S(1)}, bf16[48,1920]{1,0:T(8,128)(2,1)S(1)}, u32[]{:S(2)}, u32[]{:S(2)}) collective-permute-start(bf16[48,1920]{1,0:T(8,128)(2,1)S(1)} %copy-done.10), channel_id=1, source_target_pairs={{0,8},{1,9},{2,10},{3,11},{4,12},{5,13},{6,14},{7,15},{8,16},{9,17... | collective-permute-start | bytes 552968 | tf_op jit(solution)/shard_map/ppermute | solution.py:74
  27.2 14.7 %collective-permute-start.3 = (bf16[4,48,1280]{2,1,0:T(8,128)(2,1)S(1)}, bf16[4,48,1280]{2,1,0:T(8,128)(2,1)S(1)}, u32[]{:S(2)}, u32[]{:S(2)}) collective-permute-start(bf16[4,48,1280]{2,1,0:T(8,128)(2,1)S(1)} %pad_maximum_fusion.2.refs_0_.refs_3_), channel_id=1, source_target_pairs={{0,1},{1,0},{2,6},{3,7},{4,5},{5,4},{6,2},{7,3},{8,9},{9,8},{10,14... | collective-permute-start | bytes 1474568 | tf_op jit(solution)/shard_map/ppermute | solution.py:74
  41.4 21.4 %collective-permute-start.15 = (bf16[192,384]{1,0:T(8,128)(2,1)S(1)}, bf16[192,384]{1,0:T(8,128)(2,1)S(1)}, u32[]{:S(2)}, u32[]{:S(2)}) collective-permute-start(bf16[192,384]{1,0:T(8,128)(2,1)S(1)} %copy-done.12), channel_id=1, source_target_pairs={{0,24},{1,25},{2,26},{3,27},{4,28},{5,29},{6,30},{7,31},{8,0},{9,1... | collective-permute-start | bytes 442376 | tf_op jit(solution)/shard_map/ppermute | solution.py:74
  51.3 30.1 %collective-permute-start.20 = (bf16[4,48,1920]{2,1,0:T(8,128)(2,1)S(1)}, bf16[4,48,1920]{2,1,0:T(8,128)(2,1)S(1)}, u32[]{:S(2)}, u32[]{:S(2)}) collective-permute-start(bf16[4,48,1920]{2,1,0:T(8,128)(2,1)S(1)} %pad_maximum_fusion.refs_5_), channel_id=1, source_target_pairs={{0,1},{1,0},{2,6},{3,7},{4,5},{5,4},{6,2},{7,3},{8,9},{9,8},{10,14... | collective-permute-start | bytes 2211848 | tf_op jit(solution)/shard_map/ppermute | solution.py:74
  52.0 20.9 %collective-permute-start.16 = (bf16[4,48,1920]{2,1,0:T(8,128)(2,1)S(1)}, bf16[4,48,1920]{2,1,0:T(8,128)(2,1)S(1)}, u32[]{:S(2)}, u32[]{:S(2)}) collective-permute-start(bf16[4,48,1920]{2,1,0:T(8,128)(2,1)S(1)} %pad_maximum_fusion.refs_5_), channel_id=1, source_target_pairs={{0,4},{1,5},{2,3},{3,2},{4,0},{5,1},{6,7},{7,6},{8,12},{9,13},{10,... | collective-permute-start | bytes 2211848 | tf_op jit(solution)/shard_map/ppermute | solution.py:74
  63.1 20.0 %collective-permute-start.18 = (bf16[4,192,384]{2,1,0:T(8,128)(2,1)S(1)}, bf16[4,192,384]{2,1,0:T(8,128)(2,1)}, u32[]{:S(2)}, u32[]{:S(2)}) collective-permute-start(bf16[4,192,384]{2,1,0:T(8,128)(2,1)S(1)} %pad_maximum_fusion.1.refs_13_), channel_id=1, source_target_pairs={{0,1},{1,0},{2,6},{3,7},{4,5},{5,4},{6,2},{7,3},{8,9},{9,8},{10,14... | collective-permute-start | bytes 1769480 | tf_op jit(solution)/shard_map/ppermute | solution.py:74
  64.6 19.6 %collective-permute-start.17 = (bf16[4,192,384]{2,1,0:T(8,128)(2,1)S(1)}, bf16[4,192,384]{2,1,0:T(8,128)(2,1)}, u32[]{:S(2)}, u32[]{:S(2)}) collective-permute-start(bf16[4,192,384]{2,1,0:T(8,128)(2,1)S(1)} %pad_maximum_fusion.1.refs_13_), channel_id=1, source_target_pairs={{0,4},{1,5},{2,3},{3,2},{4,0},{5,1},{6,7},{7,6},{8,12},{9,13},{10,... | collective-permute-start | bytes 1769480 | tf_op jit(solution)/shard_map/ppermute | solution.py:74
  72.9 13.1 %collective-permute-start.19 = (bf16[4,48,1920]{2,1,0:T(8,128)(2,1)S(1)}, bf16[4,48,1920]{2,1,0:T(8,128)(2,1)S(1)}, u32[]{:S(2)}, u32[]{:S(2)}) collective-permute-start(bf16[4,48,1920]{2,1,0:T(8,128)(2,1)S(1)} %pad_maximum_fusion.refs_5_), channel_id=1, source_target_pairs={{0,2},{1,3},{2,0},{3,1},{4,6},{5,7},{6,4},{7,5},{8,10},{9,11},{10,... | collective-permute-start | bytes 2211848 | tf_op jit(solution)/shard_map/ppermute | solution.py:74
  73.0 20.8 %collective-permute-start.21 = (bf16[4,48,1920]{2,1,0:T(8,128)(2,1)S(1)}, bf16[4,48,1920]{2,1,0:T(8,128)(2,1)}, u32[]{:S(2)}, u32[]{:S(2)}) collective-permute-start(bf16[4,48,1920]{2,1,0:T(8,128)(2,1)S(1)} %collective-permute-done.16.refs_7_), channel_id=1, source_target_pairs={{0,1},{1,0},{2,6},{3,7},{4,5},{5,4},{6,2},{7,3},{8,9},{9,8},{10,14... | collective-permute-start | bytes 2211848 | tf_op jit(solution)/shard_map/ppermute | solution.py:74
  84.2 13.4 %collective-permute-start.22 = (bf16[4,192,384]{2,1,0:T(8,128)(2,1)}, bf16[4,192,384]{2,1,0:T(8,128)(2,1)}, u32[]{:S(2)}, u32[]{:S(2)}) collective-permute-start(bf16[4,192,384]{2,1,0:T(8,128)(2,1)} %collective-permute-done.17.refs_15_), channel_id=1, source_target_pairs={{0,1},{1,0},{2,6},{3,7},{4,5},{5,4},{6,2},{7,3},{8,9},{9,8},{10,14... | collective-permute-start | bytes 1769480 | tf_op jit(solution)/shard_map/ppermute | solution.py:74
  86.1 15.3 %collective-permute-start.23 = (bf16[4,48,1920]{2,1,0:T(8,128)(2,1)S(1)}, bf16[4,48,1920]{2,1,0:T(8,128)(2,1)S(1)}, u32[]{:S(2)}, u32[]{:S(2)}) collective-permute-start(bf16[4,48,1920]{2,1,0:T(8,128)(2,1)S(1)} %collective-permute-done.20.refs_6_), channel_id=1, source_target_pairs={{0,2},{1,3},{2,0},{3,1},{4,6},{5,7},{6,4},{7,5},{8,10},{9,11},{10,... | collective-permute-start | bytes 2211848 | tf_op jit(solution)/shard_map/ppermute | solution.py:74
  164.2 15.6 %collective-permute-start.30 = (bf16[2,2,4,48,1920]{4,3,2,1,0:T(8,128)(2,1)}, bf16[2,2,4,48,1920]{4,3,2,1,0:T(8,128)(2,1)}, u32[]{:S(2)}, u32[]{:S(2)}) collective-permute-start(bf16[2,2,4,48,1920]{4,3,2,1,0:T(8,128)(2,1)} %get-tuple-element.198), channel_id=1, source_target_pairs={{0,2},{1,3},{2,0},{3,1},{4,6},{5,7},{6,4},{7,5},{8,10},{9,11},{10,... | collective-permute-start | bytes 8847368 | tf_op jit(solution)/shard_map/ppermute | solution.py:74
  179.2 29.4 %collective-permute-start.35 = (bf16[2,4,192,384]{3,2,1,0:T(8,128)(2,1)}, bf16[2,4,192,384]{3,2,1,0:T(8,128)(2,1)S(1)}, u32[]{:S(2)}, u32[]{:S(2)}) collective-permute-start(bf16[2,4,192,384]{3,2,1,0:T(8,128)(2,1)} %get-tuple-element.207), channel_id=1, source_target_pairs={{0,1},{1,0},{2,6},{3,7},{4,5},{5,4},{6,2},{7,3},{8,9},{9,8},{10,14... | collective-permute-start | bytes 3538952 | tf_op jit(solution)/shard_map/ppermute | solution.py:74
  183.8 27.6 %collective-permute-start.33 = (bf16[2,4,48,1920]{3,2,1,0:T(8,128)(2,1)}, bf16[2,4,48,1920]{3,2,1,0:T(8,128)(2,1)S(1)}, u32[]{:S(2)}, u32[]{:S(2)}) collective-permute-start(bf16[2,4,48,1920]{3,2,1,0:T(8,128)(2,1)} %get-tuple-element.210), channel_id=1, source_target_pairs={{0,1},{1,0},{2,6},{3,7},{4,5},{5,4},{6,2},{7,3},{8,9},{9,8},{10,14... | collective-permute-start | bytes 4423688 | tf_op jit(solution)/shard_map/ppermute | solution.py:74
  198.9 14.3 %collective-permute-start.32 = (bf16[2,2,4,48,768]{4,3,2,1,0:T(8,128)(2,1)}, bf16[2,2,4,48,768]{4,3,2,1,0:T(8,128)(2,1)}, u32[]{:S(2)}, u32[]{:S(2)}) collective-permute-start(bf16[2,2,4,48,768]{4,3,2,1,0:T(8,128)(2,1)} %get-tuple-element.214), channel_id=1, source_target_pairs={{0,2},{1,3},{2,0},{3,1},{4,6},{5,7},{6,4},{7,5},{8,10},{9,11},{10,... | collective-permute-start | bytes 3538952 | tf_op jit(solution)/shard_map/ppermute | solution.py:74
  212.1 25.5 %collective-permute-start.38 = (bf16[4,48,1920]{2,1,0:T(8,128)(2,1)S(1)}, bf16[4,48,1920]{2,1,0:T(8,128)(2,1)S(1)}, u32[]{:S(2)}, u32[]{:S(2)}) collective-permute-start(bf16[4,48,1920]{2,1,0:T(8,128)(2,1)S(1)} %get-tuple-element.283), channel_id=1, source_target_pairs={{0,4},{1,5},{2,3},{3,2},{4,0},{5,1},{6,7},{7,6},{8,12},{9,13},{10,... | collective-permute-start | bytes 2211848 | tf_op jit(solution)/shard_map/ppermute | solution.py:74
  215.7 27.8 %collective-permute-start.34 = (bf16[2,4,48,768]{3,2,1,0:T(8,128)(2,1)}, bf16[2,4,48,768]{3,2,1,0:T(8,128)(2,1)}, u32[]{:S(2)}, u32[]{:S(2)}) collective-permute-start(bf16[2,4,48,768]{3,2,1,0:T(8,128)(2,1)} %get-tuple-element.224), channel_id=1, source_target_pairs={{0,1},{1,0},{2,6},{3,7},{4,5},{5,4},{6,2},{7,3},{8,9},{9,8},{10,14... | collective-permute-start | bytes 1769480 | tf_op jit(solution)/shard_map/ppermute | solution.py:74
  238.5 17.4 %collective-permute-start.44 = (bf16[48,1920]{1,0:T(8,128)(2,1)}, bf16[48,1920]{1,0:T(8,128)(2,1)S(1)}, u32[]{:S(2)}, u32[]{:S(2)}) collective-permute-start(bf16[48,1920]{1,0:T(8,128)(2,1)} %get-tuple-element.292), channel_id=1, source_target_pairs={{0,24},{1,25},{2,26},{3,27},{4,28},{5,29},{6,30},{7,31},{8,0},{9,1... | collective-permute-start | bytes 552968 | tf_op jit(solution)/shard_map/ppermute | solution.py:74
  239.6 17.8 %collective-permute-start.43 = (bf16[48,1920]{1,0:T(8,128)(2,1)S(1)}, bf16[48,1920]{1,0:T(8,128)(2,1)S(1)}, u32[]{:S(2)}, u32[]{:S(2)}) collective-permute-start(bf16[48,1920]{1,0:T(8,128)(2,1)S(1)} %get-tuple-element.293), channel_id=1, source_target_pairs={{0,16},{1,17},{2,18},{3,19},{4,20},{5,21},{6,22},{7,23},{8,24},{9,... | collective-permute-start | bytes 552968 | tf_op jit(solution)/shard_map/ppermute | solution.py:74
  240.4 17.1 %collective-permute-start.42 = (bf16[48,1920]{1,0:T(8,128)(2,1)S(1)}, bf16[48,1920]{1,0:T(8,128)(2,1)S(1)}, u32[]{:S(2)}, u32[]{:S(2)}) collective-permute-start(bf16[48,1920]{1,0:T(8,128)(2,1)S(1)} %get-tuple-element.294), channel_id=1, source_target_pairs={{0,8},{1,9},{2,10},{3,11},{4,12},{5,13},{6,14},{7,15},{8,16},{9,17... | collective-permute-start | bytes 552968 | tf_op jit(solution)/shard_map/ppermute | solution.py:74
  242.9 14.8 %collective-permute-start.49 = (bf16[2,4,48,512]{3,2,1,0:T(8,128)(2,1)S(1)}, bf16[2,4,48,512]{3,2,1,0:T(8,128)(2,1)S(1)}, u32[]{:S(2)}, u32[]{:S(2)}) collective-permute-start(bf16[2,4,48,512]{3,2,1,0:T(8,128)(2,1)S(1)} %get-tuple-element.287), channel_id=1, source_target_pairs={{0,1},{1,0},{2,6},{3,7},{4,5},{5,4},{6,2},{7,3},{8,9},{9,8},{10,14... | collective-permute-start | bytes 1179656 | tf_op jit(solution)/shard_map/ppermute | solution.py:74
  245.0 12.6 %collective-permute-start.45 = (bf16[4,48,768]{2,1,0:T(8,128)(2,1)S(1)}, bf16[4,48,768]{2,1,0:T(8,128)(2,1)S(1)}, u32[]{:S(2)}, u32[]{:S(2)}) collective-permute-start(bf16[4,48,768]{2,1,0:T(8,128)(2,1)S(1)} %get-tuple-element.289), channel_id=1, source_target_pairs={{0,4},{1,5},{2,3},{3,2},{4,0},{5,1},{6,7},{7,6},{8,12},{9,13},{10,... | collective-permute-start | bytes 884744 | tf_op jit(solution)/shard_map/ppermute | solution.py:74
  (65 other events, 556.9 us)

commit v3 on v1

--- a/solution.py
+++ b/solution.py
@@ -972,17 +972,17 @@
         keep_i, send_i = grad_in(pos, x, after((backward[0][0], backward[1][0]), go_d, stay_d))
         core_i = move(send_i, to_core)
         back(2, after(rows[2], keep_i))
-        low_d = add_last(*after((stay_d, second_d), backward[2]))
-        line_d = move_line(low_d)
-        go_u, stay_u = add_core(*after((stay_u, first_u), low_d))
-        second_u = move(go_u, to_second)
         parts = tuple(b[0] for b in backward)
         vbq = [b[1] for b in backward]
         vbv = [b[2] for b in backward]
+        go_u, stay_u = add_core(*after((stay_u, first_u), backward[2]))
+        second_u = move(go_u, to_second)
         go_i, stay_i = add_wide(*after((keep_i, core_i), go_u, stay_u))
         first_i = move(go_i, to_first)
+        low_d = add_last(*after((stay_d, second_d), go_i))
+        line_d = move_line(low_d)
         keep_l, send_l = grad_last(
-            pos, x, after(parts[2], go_i, stay_i), (*vbq, *vbv, vub, vob, vg1, vs1, vdb, vg2, vs2)
+            pos, x, after(parts[2], go_i, stay_i, low_d), (*vbq, *vbv, vub, vob, vg1, vs1, vdb, vg2, vs2)
         )
         core_l = move(send_l, to_core)
         mine_d = add_line(low_d, after(line_d, keep_l))

time: 288 us -> 292 us (1.014)
  transfers between devices with their start and end apart: 58 -> 58, of which waited for: 16 -> 15; matrix products, arithmetic and copies ran while one was open for 2% -> 3% of each run, Pallas kernels for 34% -> 34%
where the time goes in v3:
time: 292 us; the launch traced here: 288 us
  Pallas kernels  164 us (56%)
  waiting for transfers between devices  54.2 us (19%)
  starting transfers between devices  52.8 us (18%)
  other arithmetic  10.4 us (4%)
  local copies, waits for them, and re-layouts  5.17 us (2%)
    pallas_call x1, Pallas kernels, main_fetch(): pl.pallas_call(main_fetch_kernel, grid_spec=pltpu.PrefetchScalarGridSpec(...  61.3 us
    ppermute x58, waiting for transfers between devices, move(): return lax.ppermute(value, AXES, permutation(target))  54.2 us
    ppermute x58, starting transfers between devices, move(): return lax.ppermute(value, AXES, permutation(target))  52.8 us
    pallas_call x3, Pallas kernels, attn_bwd(): pl.pallas_call(attn_bwd_kernel, grid_spec=pltpu.PrefetchScalarGridSpec(nu...  28.7 us
    pallas_call x3, Pallas kernels, attn_fwd(): pl.pallas_call(attn_fwd_kernel, grid_spec=pltpu.PrefetchScalarGridSpec(nu...  22.8 us
    pallas_call x2, Pallas kernels, grad_call(): pl.pallas_call(kernel, grid_spec=pltpu.PrefetchScalarGridSpec(num_scalar_...  13.7 us
    pallas_call x1, Pallas kernels, ig(): pl.pallas_call(ig_fetch_kernel if fetched else ig_plain_kernel, grid_spec...  10.1 us
    pallas_call x3, Pallas kernels, add_wide(): pl.pallas_call(add_kernel, grid=(second,), in_specs=[both, both], out_spe...  10.1 us
  transfers between devices with their start and end apart: 58, of which 15 were waited for; matrix products, arithmetic and copies ran while one was open for 3% of the time, Pallas kernels for 34%

profile of v3, /device:TPU:0, one launch (start us, length us, event | category | flops | bytes accessed | tf_op | source)
XLA Modules:
  0.0 288.2 jit_solution(5771430922207199506)
XLA Ops:
  4.1 5.1 %collective-permute-start.2 = (bf16[48,1280]{1,0:T(8,128)(2,1)}, bf16[48,1280]{1,0:T(8,128)(2,1)S(1)}, u32[]{:S(2)}, u32[]{:S(2)}) collective-permute-start(bf16[48,1280]{1,0:T(8,128)(2,1)} %get-tuple-element.150), channel_id=1, source_target_pairs={{0,24},{1,25},{2,26},{3,27},{4,28},{5,29},{6,30},{7,31},{8,0},{9,1... | collective-permute-start | bytes 368648 | tf_op jit(solution)/shard_map/ppermute | solution.py:73
  13.2 6.8 %collective-permute-done.1 = bf16[48,1280]{1,0:T(8,128)(2,1)S(1)} collective-permute-done((bf16[48,1280]{1,0:T(8,128)(2,1)}, bf16[48,1280]{1,0:T(8,128)(2,1)S(1)}, u32[]{:S(2)}, u32[]{:S(2)}) %collective-permute-start.1) | collective-permute-done | bytes 122912 | tf_op jit(solution)/shard_map/ppermute | solution.py:73
  29.5 11.3 %collective-permute-done.6 = bf16[48,1920]{1,0:T(8,128)(2,1)S(1)} collective-permute-done((bf16[48,1920]{1,0:T(8,128)(2,1)S(1)}, bf16[48,1920]{1,0:T(8,128)(2,1)S(1)}, u32[]{:S(2)}, u32[]{:S(2)}) %collective-permute-start.6) | collective-permute-done | bytes 184352 | tf_op jit(solution)/shard_map/ppermute | solution.py:73
  42.0 7.7 %collective-permute-done.8.refs_3_.refs_6_ = bf16[4,48,1280]{2,1,0:T(8,128)(2,1)S(1)} collective-permute-done((bf16[4,48,1280]{2,1,0:T(8,128)(2,1)S(1)}, bf16[4,48,1280]{2,1,0:T(8,128)(2,1)S(1)}, u32[]{:S(2)}, u32[]{:S(2)}) %collective-permute-start.8) | collective-permute-done | bytes 491552 | tf_op jit(solution)/shard_map/ppermute | solution.py:73
  53.6 9.3 %qkv_fetch.1 = (bf16[1024,768]{1,0:T(8,128)(2,1)}, bf16[1024,768]{1,0:T(8,128)(2,1)}, bf16[1024,768]{1,0:T(8,128)(2,1)}, f32[1,1536]{1,0:T(1,128)}, f32[1,768]{1...) custom-call(s32[4]{0:T(128)} %pad_add_fusion.pos, ...), custom_call_target="tpu_custom_call" | custom-call | flops 11500000256 | bytes 10000000 | tf_op jit(solution)/shard_map/qkv_fetch/pallas_call | solution.py:488
  65.3 7.6 %attn_fwd.3 = (bf16[1024,256]{1,0:T(8,128)(2,1)}, f32[2,2,2,512]{3,2,1,0:T(2,128)}) custom-call(s32[2]{0:T(128)} %cnt.11, bf16[1024,768]{1,0:T(8,128)(2,1)} %get-tuple-element.171.q_ref.k_ref.v_ref, bf16[1024,768]{1,0:T(8,128)(2,1)} %get-tuple-element.171.q_ref.k_ref.v_ref, bf16[1024,768]{1,0:T(8,128)(2,1)} %get-tuple-element.171.q_ref.k_ref.v_ref), custom_call_target="tpu_custom_call" | custom-call | flops 8049999872 | bytes 7000000 | tf_op jit(solution)/shard_map/attn_fwd/pallas_call | solution.py:559
  73.8 7.6 %attn_fwd.4 = (bf16[1024,256]{1,0:T(8,128)(2,1)}, f32[2,2,2,512]{3,2,1,0:T(2,128)}) custom-call(s32[2]{0:T(128)} %cnt.11, bf16[1024,768]{1,0:T(8,128)(2,1)} %get-tuple-element.214.q_ref.k_ref.v_ref, bf16[1024,768]{1,0:T(8,128)(2,1)} %get-tuple-element.214.q_ref.k_ref.v_ref, bf16[1024,768]{1,0:T(8,128)(2,1)} %get-tuple-element.214.q_ref.k_ref.v_ref), custom_call_target="tpu_custom_call" | custom-call | flops 8049999872 | bytes 7000000 | tf_op jit(solution)/shard_map/attn_fwd/pallas_call | solution.py:559
  86.2 7.6 %attn_fwd.5 = (bf16[1024,256]{1,0:T(8,128)(2,1)}, f32[2,2,2,512]{3,2,1,0:T(2,128)}) custom-call(s32[2]{0:T(128)} %cnt.11, bf16[1024,768]{1,0:T(8,128)(2,1)} %get-tuple-element.225.q_ref.k_ref.v_ref, bf16[1024,768]{1,0:T(8,128)(2,1)} %get-tuple-element.225.q_ref.k_ref.v_ref, bf16[1024,768]{1,0:T(8,128)(2,1)} %get-tuple-element.225.q_ref.k_ref.v_ref), custom_call_target="tpu_custom_call" | custom-call | flops 8049999872 | bytes 7000000 | tf_op jit(solution)/shard_map/attn_fwd/pallas_call | solution.py:559
  94.3 3.3 %collective-permute-done.22.refs_16_ = bf16[4,192,384]{2,1,0:T(8,128)(2,1)} collective-permute-done((bf16[4,192,384]{2,1,0:T(8,128)(2,1)}, bf16[4,192,384]{2,1,0:T(8,128)(2,1)}, u32[]{:S(2)}, u32[]{:S(2)}) %collective-permute-start.22) | collective-permute-done | bytes 589856 | tf_op jit(solution)/shard_map/ppermute | solution.py:73
  98.2 3.2 %collective-permute-done.28.refs_19_ = bf16[4,192,384]{2,1,0:T(8,128)(2,1)S(1)} collective-permute-done((bf16[4,192,384]{2,1,0:T(8,128)(2,1)}, bf16[4,192,384]{2,1,0:T(8,128)(2,1)S(1)}, u32[]{:S(2)}, u32[]{:S(2)}) %collective-permute-start.28) | collective-permute-done | bytes 589856 | tf_op jit(solution)/shard_map/ppermute | solution.py:73
  102.8 61.3 %main.1 = (bf16[1024,768]{1,0:T(8,128)(2,1)}, f32[1024,768]{1,0:T(8,128)}, bf16[1024,768]{1,0:T(8,128)(2,1)}, f32[1,768]{1,0:T(1,128)}, f32[1,768]{1,0:T(1,128)}...) custom-call(s32[4]{0:T(128)} %pad_add_fusion.pos, ...), custom_call_target="tpu_custom_call" | custom-call | flops 66700001280 | bytes 58000000 | tf_op jit(solution)/shard_map/main/pallas_call | solution.py:733
  164.6 9.5 %attn_bwd.3 = (bf16[1024,768]{1,0:T(8,128)(2,1)}, f32[1,256]{1,0:T(1,128)}, f32[1,256]{1,0:T(1,128)}) custom-call(s32[2]{0:T(128)} %cnt.11, bf16[1024,768]{1,0:T(8,128)(2,1)} %get-tuple-element.171.q_ref.k_ref.v_ref, bf16[1024,768]{1,0:T(8,128)(2,1)} %get-tuple-element.171.q_ref.k_ref.v_ref, bf16[1024,768]{1,0:T(8,128)(2,1)} %get-tuple-element.171.q_ref.k_ref.v_ref, ...), custom_call_target="tpu_custom_call" | custom-call | flops 10350000128 | bytes 9000000 | tf_op jit(solution)/shard_map/attn_bwd/pallas_call | solution.py:619
  175.5 3.6 %add_wide.3 = (bf16[2,4,192,384]{3,2,1,0:T(8,128)(2,1)}, bf16[2,4,192,384]{3,2,1,0:T(8,128)(2,1)}) custom-call(bf16[2,2,4,192,384]{4,3,2,1,0:T(8,128)(2,1)} %get-tuple-element.207.keep, bf16[2,2,4,192,384]{4,3,2,1,0:T(8,128)(2,1)} %copy-done.16), custom_call_target="tpu_custom_call" | custom-call | flops 4600000000 | bytes 4000000 | tf_op jit(solution)/shard_map/add_wide/pallas_call | solution.py:108
  179.7 4.0 %add_wide.4 = (bf16[2,4,48,1920]{3,2,1,0:T(8,128)(2,1)}, bf16[2,4,48,1920]{3,2,1,0:T(8,128)(2,1)}) custom-call(bf16[2,2,4,48,1920]{4,3,2,1,0:T(8,128)(2,1)} %get-tuple-element.210.keep, bf16[2,2,4,48,1920]{4,3,2,1,0:T(8,128)(2,1)} %collective-permute-done.30.got), custom_call_target="tpu_custom_call" | custom-call | flops 4600000000 | bytes 4000000 | tf_op jit(solution)/shard_map/add_wide/pallas_call | solution.py:108
  185.1 9.6 %attn_bwd.4 = (bf16[1024,768]{1,0:T(8,128)(2,1)}, f32[1,256]{1,0:T(1,128)}, f32[1,256]{1,0:T(1,128)}) custom-call(s32[2]{0:T(128)} %cnt.11, bf16[1024,768]{1,0:T(8,128)(2,1)} %get-tuple-element.214.q_ref.k_ref.v_ref, bf16[1024,768]{1,0:T(8,128)(2,1)} %get-tuple-element.214.q_ref.k_ref.v_ref, bf16[1024,768]{1,0:T(8,128)(2,1)} %get-tuple-element.214.q_ref.k_ref.v_ref, ...), custom_call_target="tpu_custom_call" | custom-call | flops 10350000128 | bytes 9000000 | tf_op jit(solution)/shard_map/attn_bwd/pallas_call | solution.py:619
  197.4 7.3 %grad_in.1 = (bf16[2,2,4,48,768]{4,3,2,1,0:T(8,128)(2,1)}, bf16[2,2,4,48,768]{4,3,2,1,0:T(8,128)(2,1)}) custom-call(s32[4]{0:T(128)} %pad_add_fusion.pos, bf16[1024,768]{1,0:T(8,128)(2,1)} %bitcast.107, bf16[1024,768]{1,0:T(8,128)(2,1)} %get-tuple-element.221.refs_0_, bf16[1024,768]{1,0:T(8,128)(2,1)} %get-tuple-element.222.refs_1_), custom_call_target="tpu_custom_call" | custom-call | flops 5750000128 | bytes 5000000 | tf_op jit(solution)/shard_map/grad_in/pallas_call | solution.py:358
  204.7 9.6 %attn_bwd.5 = (bf16[1024,768]{1,0:T(8,128)(2,1)}, f32[1,256]{1,0:T(1,128)}, f32[1,256]{1,0:T(1,128)}) custom-call(s32[2]{0:T(128)} %cnt.11, bf16[1024,768]{1,0:T(8,128)(2,1)} %get-tuple-element.225.q_ref.k_ref.v_ref, bf16[1024,768]{1,0:T(8,128)(2,1)} %get-tuple-element.225.q_ref.k_ref.v_ref, bf16[1024,768]{1,0:T(8,128)(2,1)} %get-tuple-element.225.q_ref.k_ref.v_ref, ...), custom_call_target="tpu_custom_call" | custom-call | flops 10350000128 | bytes 9000000 | tf_op jit(solution)/shard_map/attn_bwd/pallas_call | solution.py:619
  214.3 3.4 %collective-permute-done.34 = bf16[2,4,48,1920]{3,2,1,0:T(8,128)(2,1)} collective-permute-done((bf16[2,4,48,1920]{3,2,1,0:T(8,128)(2,1)}, bf16[2,4,48,1920]{3,2,1,0:T(8,128)(2,1)}, u32[]{:S(2)}, u32[]{:S(2)}) %collective-permute-start.34) | collective-permute-done | bytes 1474592 | tf_op jit(solution)/shard_map/ppermute | solution.py:73
  225.2 3.2 %collective-permute-start.41 = (bf16[192,384]{1,0:T(8,128)(2,1)S(1)}, bf16[192,384]{1,0:T(8,128)(2,1)S(1)}, u32[]{:S(2)}, u32[]{:S(2)}) collective-permute-start(bf16[192,384]{1,0:T(8,128)(2,1)S(1)} %get-tuple-element.303), channel_id=1, source_target_pairs={{0,24},{1,25},{2,26},{3,27},{4,28},{5,29},{6,30},{7,31},{8,0},{9,1... | collective-permute-start | bytes 442376 | tf_op jit(solution)/shard_map/ppermute | solution.py:73
  229.7 6.4 %grad_last.1 = (bf16[2,2,4,48,512]{4,3,2,1,0:T(8,128)(2,1)}, bf16[2,2,4,48,512]{4,3,2,1,0:T(8,128)(2,1)}) custom-call(s32[4]{0:T(128)} %pad_add_fusion.pos, bf16[1024,768]{1,0:T(8,128)(2,1)} %bitcast.108, bf16[1024,768]{1,0:T(8,128)(2,1)} %get-tuple-element.237.part.refs_2_, f32[1,256]{1,0:T(1,128)} %get-tuple-element.205.refs_0_, ...), custom_call_target="tpu_custom_call" | custom-call | flops 4600000000 | bytes 4000000 | tf_op jit(solution)/shard_map/grad_last/pallas_call | solution.py:358
  237.6 3.5 %collective-permute-done.40 = bf16[192,384]{1,0:T(8,128)(2,1)S(1)} collective-permute-done((bf16[192,384]{1,0:T(8,128)(2,1)S(1)}, bf16[192,384]{1,0:T(8,128)(2,1)S(1)}, u32[]{:S(2)}, u32[]{:S(2)}) %collective-permute-start.40) | collective-permute-done | bytes 147488 | tf_op jit(solution)/shard_map/ppermute | solution.py:73
  250.9 10.1 %ig.1 = bf16[1024,768]{1,0:T(8,128)(2,1)} custom-call(s32[4]{0:T(128)} %pad_add_fusion.pos, f32[1024,768]{1,0:T(8,128)} %get-tuple-element.255.gf, bf16[1024,768]{1,0:T(8,128)(2,1)} %get-tuple-element.221.refs_0_, bf16[1024,768]{1,0:T(8,128)(2,1)} %get-tuple-element.222.refs_1_, bf16[1024,768]{1,0:T(8,128)(2,1)} %get-tuple-element.237.part.refs_2_, ...), custom_call_target="tpu_custom_call" | custom-call | flops 11500000256 | bytes 10000000 | tf_op jit(solution)/shard_map/ig/pallas_call | solution.py:856
  267.5 3.7 %collective-permute-done.47 = bf16[48,768]{1,0:T(8,128)(2,1)S(1)} collective-permute-done((bf16[48,768]{1,0:T(8,128)(2,1)S(1)}, bf16[48,768]{1,0:T(8,128)(2,1)S(1)}, u32[]{:S(2)}, u32[]{:S(2)}) %collective-permute-start.47) | collective-permute-done | bytes 73760 | tf_op jit(solution)/shard_map/ppermute | solution.py:73
  280.3 3.5 %collective-permute-done.57.got_last = bf16[48,512]{1,0:T(8,128)(2,1)S(1)} collective-permute-done((bf16[48,512]{1,0:T(8,128)(2,1)S(1)}, bf16[48,512]{1,0:T(8,128)(2,1)S(1)}, u32[]{:S(2)}, u32[]{:S(2)}) %collective-permute-start.57) | collective-permute-done | bytes 49184 | tf_op jit(solution)/shard_map/ppermute | solution.py:73
  (205 shorter events, 78.6 us)
Async XLA Ops:
  21.0 19.7 %collective-permute-start.4 = (bf16[4,48,1280]{2,1,0:T(8,128)(2,1)S(1)}, bf16[4,48,1280]{2,1,0:T(8,128)(2,1)S(1)}, u32[]{:S(2)}, u32[]{:S(2)}) collective-permute-start(bf16[4,48,1280]{2,1,0:T(8,128)(2,1)S(1)} %pad_maximum_fusion.2.refs_0_.refs_3_), channel_id=1, source_target_pairs={{0,4},{1,5},{2,3},{3,2},{4,0},{5,1},{6,7},{7,6},{8,12},{9,13},{10,... | collective-permute-start | bytes 1474568 | tf_op jit(solution)/shard_map/ppermute | solution.py:73
  24.3 16.4 %collective-permute-start.6 = (bf16[48,1920]{1,0:T(8,128)(2,1)S(1)}, bf16[48,1920]{1,0:T(8,128)(2,1)S(1)}, u32[]{:S(2)}, u32[]{:S(2)}) collective-permute-start(bf16[48,1920]{1,0:T(8,128)(2,1)S(1)} %copy-done.10), channel_id=1, source_target_pairs={{0,16},{1,17},{2,18},{3,19},{4,20},{5,21},{6,22},{7,23},{8,24},{9,... | collective-permute-start | bytes 552968 | tf_op jit(solution)/shard_map/ppermute | solution.py:73
  25.2 15.6 %collective-permute-start.5 = (bf16[48,1920]{1,0:T(8,128)(2,1)S(1)}, bf16[48,1920]{1,0:T(8,128)(2,1)S(1)}, u32[]{:S(2)}, u32[]{:S(2)}) collective-permute-start(bf16[48,1920]{1,0:T(8,128)(2,1)S(1)} %copy-done.10), channel_id=1, source_target_pairs={{0,8},{1,9},{2,10},{3,11},{4,12},{5,13},{6,14},{7,15},{8,16},{9,17... | collective-permute-start | bytes 552968 | tf_op jit(solution)/shard_map/ppermute | solution.py:73
  27.2 14.7 %collective-permute-start.3 = (bf16[4,48,1280]{2,1,0:T(8,128)(2,1)S(1)}, bf16[4,48,1280]{2,1,0:T(8,128)(2,1)S(1)}, u32[]{:S(2)}, u32[]{:S(2)}) collective-permute-start(bf16[4,48,1280]{2,1,0:T(8,128)(2,1)S(1)} %pad_maximum_fusion.2.refs_0_.refs_3_), channel_id=1, source_target_pairs={{0,1},{1,0},{2,6},{3,7},{4,5},{5,4},{6,2},{7,3},{8,9},{9,8},{10,14... | collective-permute-start | bytes 1474568 | tf_op jit(solution)/shard_map/ppermute | solution.py:73
  41.5 21.4 %collective-permute-start.15 = (bf16[192,384]{1,0:T(8,128)(2,1)S(1)}, bf16[192,384]{1,0:T(8,128)(2,1)S(1)}, u32[]{:S(2)}, u32[]{:S(2)}) collective-permute-start(bf16[192,384]{1,0:T(8,128)(2,1)S(1)} %copy-done.12), channel_id=1, source_target_pairs={{0,24},{1,25},{2,26},{3,27},{4,28},{5,29},{6,30},{7,31},{8,0},{9,1... | collective-permute-start | bytes 442376 | tf_op jit(solution)/shard_map/ppermute | solution.py:73
  51.3 30.1 %collective-permute-start.20 = (bf16[4,48,1920]{2,1,0:T(8,128)(2,1)S(1)}, bf16[4,48,1920]{2,1,0:T(8,128)(2,1)S(1)}, u32[]{:S(2)}, u32[]{:S(2)}) collective-permute-start(bf16[4,48,1920]{2,1,0:T(8,128)(2,1)S(1)} %pad_maximum_fusion.refs_5_), channel_id=1, source_target_pairs={{0,1},{1,0},{2,6},{3,7},{4,5},{5,4},{6,2},{7,3},{8,9},{9,8},{10,14... | collective-permute-start | bytes 2211848 | tf_op jit(solution)/shard_map/ppermute | solution.py:73
  52.0 20.9 %collective-permute-start.16 = (bf16[4,48,1920]{2,1,0:T(8,128)(2,1)S(1)}, bf16[4,48,1920]{2,1,0:T(8,128)(2,1)S(1)}, u32[]{:S(2)}, u32[]{:S(2)}) collective-permute-start(bf16[4,48,1920]{2,1,0:T(8,128)(2,1)S(1)} %pad_maximum_fusion.refs_5_), channel_id=1, source_target_pairs={{0,4},{1,5},{2,3},{3,2},{4,0},{5,1},{6,7},{7,6},{8,12},{9,13},{10,... | collective-permute-start | bytes 2211848 | tf_op jit(solution)/shard_map/ppermute | solution.py:73
  63.1 19.9 %collective-permute-start.18 = (bf16[4,192,384]{2,1,0:T(8,128)(2,1)S(1)}, bf16[4,192,384]{2,1,0:T(8,128)(2,1)}, u32[]{:S(2)}, u32[]{:S(2)}) collective-permute-start(bf16[4,192,384]{2,1,0:T(8,128)(2,1)S(1)} %pad_maximum_fusion.1.refs_13_), channel_id=1, source_target_pairs={{0,1},{1,0},{2,6},{3,7},{4,5},{5,4},{6,2},{7,3},{8,9},{9,8},{10,14... | collective-permute-start | bytes 1769480 | tf_op jit(solution)/shard_map/ppermute | solution.py:73
  64.6 19.6 %collective-permute-start.17 = (bf16[4,192,384]{2,1,0:T(8,128)(2,1)S(1)}, bf16[4,192,384]{2,1,0:T(8,128)(2,1)}, u32[]{:S(2)}, u32[]{:S(2)}) collective-permute-start(bf16[4,192,384]{2,1,0:T(8,128)(2,1)S(1)} %pad_maximum_fusion.1.refs_13_), channel_id=1, source_target_pairs={{0,4},{1,5},{2,3},{3,2},{4,0},{5,1},{6,7},{7,6},{8,12},{9,13},{10,... | collective-permute-start | bytes 1769480 | tf_op jit(solution)/shard_map/ppermute | solution.py:73
  73.0 13.1 %collective-permute-start.19 = (bf16[4,48,1920]{2,1,0:T(8,128)(2,1)S(1)}, bf16[4,48,1920]{2,1,0:T(8,128)(2,1)S(1)}, u32[]{:S(2)}, u32[]{:S(2)}) collective-permute-start(bf16[4,48,1920]{2,1,0:T(8,128)(2,1)S(1)} %pad_maximum_fusion.refs_5_), channel_id=1, source_target_pairs={{0,2},{1,3},{2,0},{3,1},{4,6},{5,7},{6,4},{7,5},{8,10},{9,11},{10,... | collective-permute-start | bytes 2211848 | tf_op jit(solution)/shard_map/ppermute | solution.py:73
  73.0 20.8 %collective-permute-start.21 = (bf16[4,48,1920]{2,1,0:T(8,128)(2,1)S(1)}, bf16[4,48,1920]{2,1,0:T(8,128)(2,1)}, u32[]{:S(2)}, u32[]{:S(2)}) collective-permute-start(bf16[4,48,1920]{2,1,0:T(8,128)(2,1)S(1)} %collective-permute-done.16.refs_7_), channel_id=1, source_target_pairs={{0,1},{1,0},{2,6},{3,7},{4,5},{5,4},{6,2},{7,3},{8,9},{9,8},{10,14... | collective-permute-start | bytes 2211848 | tf_op jit(solution)/shard_map/ppermute | solution.py:73
  84.2 13.4 %collective-permute-start.22 = (bf16[4,192,384]{2,1,0:T(8,128)(2,1)}, bf16[4,192,384]{2,1,0:T(8,128)(2,1)}, u32[]{:S(2)}, u32[]{:S(2)}) collective-permute-start(bf16[4,192,384]{2,1,0:T(8,128)(2,1)} %collective-permute-done.17.refs_15_), channel_id=1, source_target_pairs={{0,1},{1,0},{2,6},{3,7},{4,5},{5,4},{6,2},{7,3},{8,9},{9,8},{10,14... | collective-permute-start | bytes 1769480 | tf_op jit(solution)/shard_map/ppermute | solution.py:73
  86.1 15.3 %collective-permute-start.23 = (bf16[4,48,1920]{2,1,0:T(8,128)(2,1)S(1)}, bf16[4,48,1920]{2,1,0:T(8,128)(2,1)S(1)}, u32[]{:S(2)}, u32[]{:S(2)}) collective-permute-start(bf16[4,48,1920]{2,1,0:T(8,128)(2,1)S(1)} %collective-permute-done.20.refs_6_), channel_id=1, source_target_pairs={{0,2},{1,3},{2,0},{3,1},{4,6},{5,7},{6,4},{7,5},{8,10},{9,11},{10,... | collective-permute-start | bytes 2211848 | tf_op jit(solution)/shard_map/ppermute | solution.py:73
  164.0 15.6 %collective-permute-start.30 = (bf16[2,2,4,48,1920]{4,3,2,1,0:T(8,128)(2,1)}, bf16[2,2,4,48,1920]{4,3,2,1,0:T(8,128)(2,1)}, u32[]{:S(2)}, u32[]{:S(2)}) collective-permute-start(bf16[2,2,4,48,1920]{4,3,2,1,0:T(8,128)(2,1)} %get-tuple-element.202), channel_id=1, source_target_pairs={{0,2},{1,3},{2,0},{3,1},{4,6},{5,7},{6,4},{7,5},{8,10},{9,11},{10,... | collective-permute-start | bytes 8847368 | tf_op jit(solution)/shard_map/ppermute | solution.py:73
  179.1 16.4 %collective-permute-start.32 = (bf16[2,4,192,384]{3,2,1,0:T(8,128)(2,1)}, bf16[2,4,192,384]{3,2,1,0:T(8,128)(2,1)S(1)}, u32[]{:S(2)}, u32[]{:S(2)}) collective-permute-start(bf16[2,4,192,384]{3,2,1,0:T(8,128)(2,1)} %get-tuple-element.209), channel_id=1, source_target_pairs={{0,1},{1,0},{2,6},{3,7},{4,5},{5,4},{6,2},{7,3},{8,9},{9,8},{10,14... | collective-permute-start | bytes 3538952 | tf_op jit(solution)/shard_map/ppermute | solution.py:73
  183.7 34.0 %collective-permute-start.34 = (bf16[2,4,48,1920]{3,2,1,0:T(8,128)(2,1)}, bf16[2,4,48,1920]{3,2,1,0:T(8,128)(2,1)}, u32[]{:S(2)}, u32[]{:S(2)}) collective-permute-start(bf16[2,4,48,1920]{3,2,1,0:T(8,128)(2,1)} %get-tuple-element.212), channel_id=1, source_target_pairs={{0,1},{1,0},{2,6},{3,7},{4,5},{5,4},{6,2},{7,3},{8,9},{9,8},{10,14... | collective-permute-start | bytes 4423688 | tf_op jit(solution)/shard_map/ppermute | solution.py:73
  196.2 27.7 %collective-permute-start.36 = (bf16[4,192,384]{2,1,0:T(8,128)(2,1)S(1)}, bf16[4,192,384]{2,1,0:T(8,128)(2,1)}, u32[]{:S(2)}, u32[]{:S(2)}) collective-permute-start(bf16[4,192,384]{2,1,0:T(8,128)(2,1)S(1)} %get-tuple-element.289), channel_id=1, source_target_pairs={{0,4},{1,5},{2,3},{3,2},{4,0},{5,1},{6,7},{7,6},{8,12},{9,13},{10,... | collective-permute-start | bytes 1769480 | tf_op jit(solution)/shard_map/ppermute | solution.py:73
  204.7 16.3 %collective-permute-start.33 = (bf16[2,2,4,48,768]{4,3,2,1,0:T(8,128)(2,1)}, bf16[2,2,4,48,768]{4,3,2,1,0:T(8,128)(2,1)}, u32[]{:S(2)}, u32[]{:S(2)}) collective-permute-start(bf16[2,2,4,48,768]{4,3,2,1,0:T(8,128)(2,1)} %get-tuple-element.224), channel_id=1, source_target_pairs={{0,2},{1,3},{2,0},{3,1},{4,6},{5,7},{6,4},{7,5},{8,10},{9,11},{10,... | collective-permute-start | bytes 3538952 | tf_op jit(solution)/shard_map/ppermute | solution.py:73
  219.8 21.4 %collective-permute-start.38 = (bf16[4,48,1920]{2,1,0:T(8,128)(2,1)S(1)}, bf16[4,48,1920]{2,1,0:T(8,128)(2,1)S(1)}, u32[]{:S(2)}, u32[]{:S(2)}) collective-permute-start(bf16[4,48,1920]{2,1,0:T(8,128)(2,1)S(1)} %get-tuple-element.287), channel_id=1, source_target_pairs={{0,4},{1,5},{2,3},{3,2},{4,0},{5,1},{6,7},{7,6},{8,12},{9,13},{10,... | collective-permute-start | bytes 2211848 | tf_op jit(solution)/shard_map/ppermute | solution.py:73
  223.4 24.7 %collective-permute-start.35 = (bf16[2,4,48,768]{3,2,1,0:T(8,128)(2,1)}, bf16[2,4,48,768]{3,2,1,0:T(8,128)(2,1)}, u32[]{:S(2)}, u32[]{:S(2)}) collective-permute-start(bf16[2,4,48,768]{3,2,1,0:T(8,128)(2,1)} %get-tuple-element.234), channel_id=1, source_target_pairs={{0,1},{1,0},{2,6},{3,7},{4,5},{5,4},{6,2},{7,3},{8,9},{9,8},{10,14... | collective-permute-start | bytes 1769480 | tf_op jit(solution)/shard_map/ppermute | solution.py:73
  242.1 19.0 %collective-permute-start.44 = (bf16[48,1920]{1,0:T(8,128)(2,1)}, bf16[48,1920]{1,0:T(8,128)(2,1)S(1)}, u32[]{:S(2)}, u32[]{:S(2)}) collective-permute-start(bf16[48,1920]{1,0:T(8,128)(2,1)} %get-tuple-element.296), channel_id=1, source_target_pairs={{0,24},{1,25},{2,26},{3,27},{4,28},{5,29},{6,30},{7,31},{8,0},{9,1... | collective-permute-start | bytes 552968 | tf_op jit(solution)/shard_map/ppermute | solution.py:73
  242.4 18.7 %collective-permute-start.43 = (bf16[48,1920]{1,0:T(8,128)(2,1)S(1)}, bf16[48,1920]{1,0:T(8,128)(2,1)S(1)}, u32[]{:S(2)}, u32[]{:S(2)}) collective-permute-start(bf16[48,1920]{1,0:T(8,128)(2,1)S(1)} %get-tuple-element.297), channel_id=1, source_target_pairs={{0,16},{1,17},{2,18},{3,19},{4,20},{5,21},{6,22},{7,23},{8,24},{9,... | collective-permute-start | bytes 552968 | tf_op jit(solution)/shard_map/ppermute | solution.py:73
  243.9 17.2 %collective-permute-start.42 = (bf16[48,1920]{1,0:T(8,128)(2,1)S(1)}, bf16[48,1920]{1,0:T(8,128)(2,1)S(1)}, u32[]{:S(2)}, u32[]{:S(2)}) collective-permute-start(bf16[48,1920]{1,0:T(8,128)(2,1)S(1)} %get-tuple-element.298), channel_id=1, source_target_pairs={{0,8},{1,9},{2,10},{3,11},{4,12},{5,13},{6,14},{7,15},{8,16},{9,17... | collective-permute-start | bytes 552968 | tf_op jit(solution)/shard_map/ppermute | solution.py:73
  246.5 14.8 %collective-permute-start.49 = (bf16[2,4,48,512]{3,2,1,0:T(8,128)(2,1)S(1)}, bf16[2,4,48,512]{3,2,1,0:T(8,128)(2,1)S(1)}, u32[]{:S(2)}, u32[]{:S(2)}) collective-permute-start(bf16[2,4,48,512]{3,2,1,0:T(8,128)(2,1)S(1)} %get-tuple-element.291), channel_id=1, source_target_pairs={{0,1},{1,0},{2,6},{3,7},{4,5},{5,4},{6,2},{7,3},{8,9},{9,8},{10,14... | collective-permute-start | bytes 1179656 | tf_op jit(solution)/shard_map/ppermute | solution.py:73
  (65 other events, 573.0 us)
